TPU v7x, 32 devices: a whole 2x2x4 slice. The times are simulated.
32 devices in a mesh: grp: 2 (over x), beam: 8 (over z, y), tp: 2 (over core).
Axes of the slice: x: 2, y: 2, z: 4, core: 2. Of those that a mesh axis runs over, the one named last changes fastest.
Arguments:
- queries: bfloat16 [256, 20, 128], P(('grp', 'beam'), 'tp'), parts along dimension 0, may hold values from -48 to 48
- new_entries: bfloat16 [256, 2, 4, 128], P(('grp', 'beam'), None, 'tp'), parts along dimension 0, may hold values from -6 to 6
- cache_pages: bfloat16 [768, 2, 4, 128, 128], P(('grp', 'beam'), None, 'tp'), parts along dimension 0, may hold values from -6 to 6
- cache_scales: bfloat16 [768, 2, 4], P(('grp', 'beam'), None, 'tp'), parts along dimension 0, may hold values from 0.5 to 2
- page_table: int32 [256, 3], P(('grp', 'beam')), parts along dimension 0, may hold values from 0 to 47, as said below
- lengths: int32 [256], P('grp'), parts along dimension 0, may hold values from 256 to 384, as said below
- parent: int32 [256], P('grp'), parts along dimension 0, may hold values from 0 to 127, as said below
- placement: int32 [256], P('grp'), parts along dimension 0, may hold values from 0 to 127, as said below
- out_weight: bfloat16 [2560, 2560], P('tp'), may hold values from -0.125 to 0.125
Outputs:
- mixed: bfloat16 [256, 2560], P(('grp', 'beam'), 'tp'), parts along dimension 0
There are 2 independent parts, one for each index of `grp`. A program takes and returns all parts, laid end to end along the dimension named above; an argument that names none is the same for every part. Nothing has to cross between parts.
Inputs may be any that keep to these rules, and one draw needn't show every extreme that they name: `placement`: a permutation: each parent beam in its own slot. Among the children in the slots of one index of beam, at most 2 have their parent's slot on any one index of beam, and exactly 2 on some index; children may share a parent. `lengths`: multiples of 128; every index of beam holds a beam of length 384. `page_table`: the rows of the slots of one index of beam hold each of its page numbers 0 to 47 once.
All inputs are finite; a program needn't handle non-finite values.
Results may differ from a plain program's by a relative error of at most 0.0053.
Values may be sent and summed in bfloat16 or wider, within the bound.
No kernel may reach another device: no remote copies, remote signals or barrier semaphores. Data moves between devices by JAX's collectives and lax.ppermute only.
A program may use at most 128 MiB of HBM per device.

v0:
```python
import math

import jax
import jax.numpy as jnp
from jax import lax
from jax.sharding import PartitionSpec as P


def attend(queries, entries, page_blocks, scales, lengths):
    item_count, head_count, head_size = queries.shape
    key_heads = entries.shape[2]
    group_size = head_count // key_heads
    page_limit = page_blocks.shape[1]
    page_rows = page_blocks.shape[4]
    factor = 1.0 / math.sqrt(head_size)
    grouped = queries.reshape(item_count, key_heads, group_size, head_size)
    scale_values = scales.astype(jnp.float32)
    raw_scores = jnp.einsum(
        "nkgd,npktd->nkgpt", grouped, page_blocks[:, :, 0], preferred_element_type=jnp.float32
    )
    key_scale = jnp.transpose(scale_values[:, :, 0], (0, 2, 1))[:, :, None, :, None]
    scores = raw_scores * key_scale * factor
    position = jnp.arange(page_limit * page_rows, dtype=jnp.int32).reshape(page_limit, page_rows)
    visible = position[None, None, None] < lengths[:, None, None, None, None]
    scores = jnp.where(visible, scores, -jnp.inf)
    fresh_score = (
        jnp.einsum("nkgd,nkd->nkg", grouped, entries[:, 0], preferred_element_type=jnp.float32)
        * factor
    )
    highest = jnp.maximum(jnp.max(scores, axis=(3, 4)), fresh_score)
    weights = jnp.where(visible, jnp.exp(scores - highest[..., None, None]), 0.0)
    fresh_weight = jnp.exp(fresh_score - highest)
    denominator = jnp.sum(weights, axis=(3, 4)) + fresh_weight
    rounded = weights.astype(jnp.bfloat16)
    fresh_rounded = fresh_weight.astype(jnp.bfloat16)
    blocks = jnp.einsum(
        "nkgpt,npktd->nkgpd", rounded, page_blocks[:, :, 1], preferred_element_type=jnp.float32
    )
    value_scale = jnp.transpose(scale_values[:, :, 1], (0, 2, 1))[:, :, None, :, None]
    summed = jnp.sum(blocks * value_scale, axis=3)
    summed = summed + jnp.einsum(
        "nkg,nkd->nkgd", fresh_rounded, entries[:, 1], preferred_element_type=jnp.float32
    )
    attended = summed / denominator[..., None]
    return attended.reshape(item_count, head_count * head_size).astype(jnp.bfloat16)


def on_device(
    queries,
    new_entries,
    cache_pages,
    cache_scales,
    page_table,
    lengths,
    parent,
    placement,
    out_weight,
):
    beam_count = lax.axis_size("beam")
    own_index = lax.axis_index("beam")
    per_device = queries.shape[0]
    page_limit = page_table.shape[1]
    slot_count = (per_device + beam_count - 1) // beam_count
    parent_slot = placement[parent]
    source = (parent_slot // per_device).reshape(beam_count, per_device)
    local_slot = (parent_slot % per_device).reshape(beam_count, per_device)
    devices = jnp.arange(beam_count, dtype=jnp.int32)
    member = (source[:, :, None] == devices[None, None, :]).astype(jnp.int32)
    earlier = jnp.cumsum(member, axis=1) - member
    order_rank = jnp.sum(earlier * member, axis=2)
    own_source = lax.dynamic_index_in_dim(source, own_index, 0, keepdims=False)
    own_rank = lax.dynamic_index_in_dim(order_rank, own_index, 0, keepdims=False)
    own_rows = own_source * slot_count + own_rank
    own_parents = lax.dynamic_slice_in_dim(parent_slot, own_index * per_device, per_device)
    own_lengths = lengths[own_parents]
    wanted = (source == own_index)[:, :, None] & (
        order_rank[:, :, None] == jnp.arange(slot_count, dtype=jnp.int32)[None, None, :]
    )
    serve_slot = jnp.sum(jnp.where(wanted, local_slot[:, :, None], 0), axis=1).reshape(
        beam_count * slot_count
    )
    flat_pages = page_table[serve_slot].reshape(beam_count * slot_count * page_limit)
    outgoing = cache_pages[flat_pages].reshape(
        (beam_count * slot_count, page_limit) + cache_pages.shape[1:]
    )
    outgoing_scales = cache_scales[flat_pages].reshape(
        (beam_count * slot_count, page_limit) + cache_scales.shape[1:]
    )
    arrived, arrived_scales = (
        lax.all_to_all(outgoing, "beam", split_axis=0, concat_axis=0, tiled=True),
        lax.all_to_all(outgoing_scales, "beam", split_axis=0, concat_axis=0, tiled=True),
    )
    attended = attend(
        queries, new_entries, arrived[own_rows], arrived_scales[own_rows], own_lengths
    )
    partial_value = jnp.dot(attended, out_weight, preferred_element_type=jnp.float32)
    summed = lax.psum(partial_value, "tp")
    col_width = partial_value.shape[1] // lax.axis_size("tp")
    own_columns = lax.dynamic_slice_in_dim(summed, lax.axis_index("tp") * col_width, col_width, 1)
    return own_columns.astype(jnp.bfloat16)


def solution(mesh):
    return jax.shard_map(
        on_device,
        mesh=mesh,
        in_specs=(
            P(("grp", "beam"), "tp", None),
            P(("grp", "beam"), None, "tp", None),
            P(("grp", "beam"), None, "tp", None, None),
            P(("grp", "beam"), None, "tp"),
            P(("grp", "beam"), None),
            P("grp"),
            P("grp"),
            P("grp"),
            P("tp", None),
        ),
        out_specs=P(("grp", "beam"), "tp"),
        check_vma=False,
    )
```

profile of v0, /device:TPU:0, one launch (start us, length us, event | category | flops | bytes accessed | tf_op | source)
XLA Modules:
  0.0 187.6 jit_solution(5130102797580314308)
XLA Ops:
  0.0 0.7 compare_select_fusion.4
  0.7 1.2 gather_fusion
  1.9 0.1 gather.24
  2.0 0.1 copy.82
  2.1 0.4 fusion.33
  2.6 0.1 select_reduce_fusion
  2.7 0.1 copy.84
  2.8 0.1 reshape.192
  2.9 0.8 copy.85
  3.7 0.6 gather_fusion.1
  4.3 0.1 reshape.193
  4.4 0.8 copy.90
  5.2 0.6 gather_fusion.5
  5.8 0.9 copy.92
  6.7 7.3 %all-to-all-start.1 = ((bf16[16,3,2,2]{1,3,2,0:T(2,128)(2,1)}), bf16[16,3,2,2]{1,3,2,0:T(2,128)(2,1)S(1)}, u32[]{:S(2)}, u32[]{:S(2)}) async-start(bf16[16,3,2,2]{1,3,2,0:T(2,128)(2,1)} %copy.92), calls=%async_computation.1 | async-start | bytes 32768 | tf_op jit(solution)/shard_map/all_to_all | solution.py:91
  14.0 7.8 %gather_fusion.2 = bf16[48,2,2,128,128]{4,3,2,1,0:T(8,128)(2,1)} fusion(bf16[48,2,2,128,128]{4,3,2,1,0:T(8,128)(2,1)} %param.11, s32[1024]{0:T(1024)S(1)} %pad_clamp_fusion.2), kind=kCustom, calls=%fused_computation.2 | custom fusion | bytes 12583104 | tf_op jit(solution)/shard_map/gather | solution.py:83
  21.7 6.1 %all-to-all-start = ((bf16[16,3,2,2,128,128]{5,4,3,2,1,0:T(8,128)(2,1)}), bf16[16,3,2,2,128,128]{5,4,3,2,1,0:T(8,128)(2,1)}, u32[]{:S(2)}, u32[]{:S(2)}) async-start(bf16[16,3,2,2,128,128]{5,4,3,2,1,0:T(8,128)(2,1)} %bitcast.64), calls=%async_computation | async-start | bytes 12582912 | tf_op jit(solution)/shard_map/all_to_all | solution.py:90
  27.9 0.1 compare_select_fusion
  28.0 0.7 gather_fusion.4
  28.7 0.1 broadcast_compare_fusion
  28.8 0.2 fusion.17
  29.0 0.6 gather_fusion.6
  29.6 135.9 %all-to-all-done = bf16[16,3,2,2,128,128]{5,4,3,2,1,0:T(8,128)(2,1)} async-done(((bf16[16,3,2,2,128,128]{5,4,3,2,1,0:T(8,128)(2,1)}), bf16[16,3,2,2,128,128]{5,4,3,2,1,0:T(8,128)(2,1)}, u32[]{:S(2)}, u32[]{:S(2)}) %all-to-all-start) | async-done | bytes 6291488 | tf_op jit(solution)/shard_map/all_to_all | solution.py:90
  165.5 6.8 %gather_fusion.3 = bf16[16,3,2,2,128,128]{5,4,3,2,1,0:T(8,128)(2,1)} fusion(bf16[16,3,2,2,128,128]{5,4,3,2,1,0:T(8,128)(2,1)} %all-to-all-done, s32[1024]{0:T(1024)S(1)} %pad_clamp_fusion.1), kind=kCustom, calls=%fused_computation.3 | custom fusion | bytes 12582976 | tf_op jit(solution)/shard_map/gather | solution.py:94
  172.3 4.2 %fusion.32 = (bf16[16,3,1,2,128,128]{5,4,3,2,1,0:T(8,128)(2,1)S(1)}, bf16[16,3,1,2,128,128]{5,4,3,2,1,0:T(8,128)(2,1)S(1)}) fusion(bf16[16,3,2,2,128,128]{5,4,3,2,1,0:T(8,128)(2,1)} %gather_fusion.3), kind=kLoop, calls=%fused_computation.76 | loop fusion | bytes 12582912 | tf_op jit(solution)/shard_map/slice | solution.py:19
  176.5 1.3 fusion.34
  177.9 0.2 fusion.9
  178.1 1.0 fusion.7
  179.1 0.1 fusion.16
  179.4 3.8 %fusion.35 = f32[16,2560]{1,0:T(8,128)S(1)} fusion(bf16[16,1280]{1,0:T(8,128)(2,1)S(1)} %convert_element_type.26, bf16[1280,2560]{1,0:T(8,128)(2,1)} %param.17), kind=kOutput, calls=%fused_computation.79 | convolution fusion | flops 104857600 | bytes 6758400 | tf_op jit(solution)/shard_map/dot_general | solution.py:96
  183.2 3.8 %all-reduce.1 = bf16[16,2560]{1,0:T(8,128)(2,1)S(1)} all-reduce(f32[16,2560]{1,0:T(8,128)S(1)} %fusion.35), channel_id=1, replica_groups=mesh['grp'=2,'beam'=8,'tp'=2] {'tp'}, use_global_device_ids=true, to_apply=%region_6.7 | all-reduce | flops 40960 | bytes 245760 | tf_op jit(solution)/shard_map/psum | solution.py:97
  187.0 0.6 dynamic-slice_convert_fusion
  (27 shorter events, 0.3 us)
Async XLA Ops:
  0.0 0.7 copy-start
  6.7 15.0 %all-to-all-start.1 = ((bf16[16,3,2,2]{1,3,2,0:T(2,128)(2,1)}), bf16[16,3,2,2]{1,3,2,0:T(2,128)(2,1)S(1)}, u32[]{:S(2)}, u32[]{:S(2)}) async-start(bf16[16,3,2,2]{1,3,2,0:T(2,128)(2,1)} %copy.92), calls=%async_computation.1 | async-start | bytes 32768 | tf_op jit(solution)/shard_map/all_to_all | solution.py:91
  21.7 6.2 %copy-start.1 = (s32[128]{0:T(128)S(1)}, s32[128]{0:T(128)}, u32[]{:S(2)}) copy-start(s32[128]{0:T(128)} %param.14) | copy-start | bytes 1540
  21.7 7.0 %copy-start.2 = (bf16[16,2,2,128]{3,2,1,0:T(2,128)(2,1)S(1)}, bf16[16,2,2,128]{3,2,1,0:T(2,128)(2,1)}, u32[]{:S(2)}) copy-start(bf16[16,2,2,128]{3,2,1,0:T(2,128)(2,1)} %param.10) | copy-start | bytes 49156
  21.7 7.0 %copy-start.3 = (bf16[16,10,128]{2,0,1:T(8,128)(2,1)S(1)}, bf16[16,10,128]{2,0,1:T(8,128)(2,1)}, u32[]{:S(2)}) copy-start(bf16[16,10,128]{2,0,1:T(8,128)(2,1)} %param.9) | copy-start | bytes 122884
  21.7 143.8 %all-to-all-start = ((bf16[16,3,2,2,128,128]{5,4,3,2,1,0:T(8,128)(2,1)}), bf16[16,3,2,2,128,128]{5,4,3,2,1,0:T(8,128)(2,1)}, u32[]{:S(2)}, u32[]{:S(2)}) async-start(bf16[16,3,2,2,128,128]{5,4,3,2,1,0:T(8,128)(2,1)} %bitcast.64), calls=%async_computation | async-start | bytes 12582912 | tf_op jit(solution)/shard_map/all_to_all | solution.py:90
where the time goes:
time: 188 us
  waiting for transfers between devices  136 us (72%)
  local copies, waits for them, and re-layouts  26.1 us (14%)
  starting transfers between devices  13.4 us (7%)
  matrix products  6.26 us (3%)
  blocking collectives  3.83 us (2%)
  other arithmetic  1.95 us (1%)
    all_to_all x1, waiting for transfers between devices, on_device(): lax.all_to_all(outgoing, 'beam', split_axis=0, concat_axis=0, tiled=True)  136 us
    gather x1, local copies, waits for them, and re-layouts, on_device(): cache_pages[flat_pages]  7.75 us
    all_to_all x1, starting transfers between devices, on_device(): lax.all_to_all(outgoing_scales, 'beam', split_axis=0, concat_axis=0, tile...  7.28 us
    gather x1, local copies, waits for them, and re-layouts, on_device(): arrived[own_rows]  6.79 us
    all_to_all x1, starting transfers between devices, on_device(): lax.all_to_all(outgoing, 'beam', split_axis=0, concat_axis=0, tiled=True)  6.12 us
    slice x1, local copies, waits for them, and re-layouts, attend(): page_blocks[:, :, 0]  4.21 us
    psum x1, blocking collectives, on_device(): summed = lax.psum(partial_value, 'tp')  3.83 us
    dot_general x1, matrix products, on_device(): jnp.dot(attended, out_weight, preferred_element_type=jnp.float32)  3.82 us
  transfers between devices with their start and end apart: 2, of which 1 were waited for; matrix products, arithmetic and copies ran while one was open for 5% of the time, Pallas kernels for 0%

commit v1 on v0

v1 whole, which is shorter than its diff:
```python
import functools
import math

import jax
import jax.numpy as jnp
from jax import lax
from jax.experimental import pallas as pl
from jax.experimental.pallas import tpu as pltpu
from jax.sharding import PartitionSpec as P

ITEM_ROWS = 16
VMEM = pltpu.VMEM
SMEM = pltpu.SMEM


def pack_kernel(
    beams,
    slots,
    parent_ref,
    placement_ref,
    query_ref,
    entry_ref,
    scale_ref,
    send_ref,
    select_ref,
    scale_out_ref,
    count_ref,
):
    heads, children, head_size = query_ref.shape
    entry_rows = entry_ref.shape[0]
    per_child = entry_rows // children
    own = lax.axis_index("beam")
    scale_out_ref[...] = scale_ref[...].astype(jnp.float32)
    for index in range(beams):
        count_ref[index] = 0
    query_lane = lax.broadcasted_iota(jnp.int32, (8, heads * children), 1)
    entry_lane = lax.broadcasted_iota(jnp.int32, (8, entry_rows), 1)
    query_child = query_lane % children
    entry_child = entry_lane // per_child
    query_row = query_lane // children
    entry_row = entry_lane % per_child + heads
    select_shape = select_ref.shape
    child_row = lax.broadcasted_iota(jnp.int32, select_shape, 0)
    select_lane = lax.broadcasted_iota(jnp.int32, select_shape, 1)
    select_item = (select_lane // (2 * slots)) * slots + select_lane % slots
    select = jnp.zeros(select_shape, jnp.int32)
    for child in range(children):
        slot = placement_ref[parent_ref[own * children + child]]
        source = slot // children
        rank = count_ref[source]
        count_ref[source] = rank + 1
        item = source * slots + rank
        query_row = jnp.where(query_child == child, query_row + item * ITEM_ROWS, query_row)
        entry_row = jnp.where(entry_child == child, entry_row + item * ITEM_ROWS, entry_row)
        select = jnp.where((child_row == child) & (select_item == item), 1, select)
    select_ref[...] = select.astype(jnp.float32).astype(jnp.bfloat16)
    rows = beams * slots * ITEM_ROWS
    row_of = lax.broadcasted_iota(jnp.int32, (rows, heads * children), 0)
    pick = (row_of == query_row[:1]).astype(jnp.float32).astype(jnp.bfloat16)
    entry_row_of = lax.broadcasted_iota(jnp.int32, (rows, entry_rows), 0)
    entry_pick = (entry_row_of == entry_row[:1]).astype(jnp.float32).astype(jnp.bfloat16)
    moved = jnp.dot(
        pick, query_ref[...].reshape(heads * children, head_size), preferred_element_type=jnp.float32
    )
    moved += jnp.dot(entry_pick, entry_ref[...], preferred_element_type=jnp.float32)
    send_ref[...] = moved.astype(jnp.bfloat16).reshape(send_ref.shape)


def route_kernel(
    beams,
    slots,
    children,
    parent_ref,
    placement_ref,
    table_ref,
    length_ref,
    page_ref,
    item_length_ref,
):
    own = lax.axis_index("beam")
    page_limit = table_ref.shape[0]

    def clear(item, _):
        item_length_ref[item] = length_ref[own * children]
        for page in range(page_limit):
            page_ref[item * page_limit + page] = table_ref[page, 0]
        return 0

    lax.fori_loop(0, beams * slots, clear, 0)

    def one_index(index, _):
        def one_child(child, rank):
            slot = placement_ref[parent_ref[index * children + child]]
            mine = slot // children == own

            @pl.when(mine)
            def _():
                item = index * slots + rank
                item_length_ref[item] = length_ref[slot]
                for page in range(page_limit):
                    page_ref[item * page_limit + page] = table_ref[page, slot % children]

            return rank + mine.astype(jnp.int32)

        lax.fori_loop(0, children, one_child, 0, unroll=4)
        return 0

    lax.fori_loop(0, beams, one_index, 0)


def attend_kernel(
    slots,
    factor,
    page_ref,
    item_length_ref,
    scale_ref,
    arrived_ref,
    pages_ref,
    weight_ref,
    out_ref,
    attended_ref,
):
    item_count = arrived_ref.shape[0]
    page_count, _, key_heads, page_rows, head_size = pages_ref.shape
    page_limit = page_ref.shape[0] // item_count
    heads = weight_ref.shape[0] // head_size
    group = heads // key_heads
    row = lax.broadcasted_iota(jnp.int32, (ITEM_ROWS, head_size), 0)
    row_head = [(row >= head * group) & (row < (head + 1) * group) for head in range(key_heads)]
    column = row[:, :1]
    column_head = [(column >= head * group) & (column < (head + 1) * group) for head in range(key_heads)]

    def by_head(masks, parts):
        result = jnp.zeros((), jnp.float32)
        for mask, part in zip(masks, parts):
            result = jnp.where(mask, part, result)
        return result

    for item in range(item_count):
        packed = arrived_ref[item].astype(jnp.float32)
        wide = jnp.concatenate([jnp.where(mask, packed, 0.0) for mask in row_head], axis=1).astype(jnp.bfloat16)
        length = item_length_ref[item]
        numbers = [page_ref[item * page_limit + page] for page in range(page_limit)]
        scores = []
        for page, number in enumerate(numbers):
            keys = jnp.concatenate([pages_ref[number, 0, head] for head in range(key_heads)], axis=1)
            raw = lax.dot_general(wide, keys, (((1,), (1,)), ((), ())), preferred_element_type=jnp.float32)
            key_scale = by_head(column_head, [scale_ref[head, number] * factor for head in range(key_heads)])
            hidden = jnp.where(page * page_rows < length, 0.0, -jnp.inf)
            scores.append(raw * key_scale + hidden)
        fresh_key = by_head(row_head, [packed[heads + head][None] for head in range(key_heads)])
        fresh_value = by_head(row_head, [packed[heads + key_heads + head][None] for head in range(key_heads)])
        fresh = jnp.sum(packed * fresh_key, axis=1, keepdims=True) * factor
        highest = jnp.maximum(jnp.max(functools.reduce(jnp.maximum, scores), axis=1, keepdims=True), fresh)
        fresh_weight = jnp.exp(fresh - highest)
        total = jnp.zeros((), jnp.float32)
        summed = fresh_weight.astype(jnp.bfloat16).astype(jnp.float32) * fresh_value
        for number, score in zip(numbers, scores):
            weights = jnp.exp(score - highest)
            total = total + weights
            values = jnp.concatenate([pages_ref[number, 1, head] for head in range(key_heads)], axis=1)
            product = jnp.dot(weights.astype(jnp.bfloat16), values, preferred_element_type=jnp.float32)
            summed = summed + by_head(
                row_head,
                [
                    product[:, head * head_size : (head + 1) * head_size] * scale_ref[key_heads + head, number]
                    for head in range(key_heads)
                ],
            )
        denominator = jnp.sum(total, axis=1, keepdims=True) + fresh_weight
        attended_ref[item * ITEM_ROWS : (item + 1) * ITEM_ROWS, :] = summed / denominator
    attended = jnp.concatenate(
        [attended_ref[pl.ds(head, item_count, stride=ITEM_ROWS), :] for head in range(heads)], axis=1
    ).astype(jnp.bfloat16)
    width = out_ref.shape[2]
    for half in range(2):
        part = jnp.dot(
            attended, weight_ref[:, half * width : (half + 1) * width], preferred_element_type=jnp.float32
        ).astype(jnp.bfloat16)
        for index in range(item_count // slots):
            out_ref[index * 2 + half] = part[index * slots : (index + 1) * slots]


def finish_kernel(select_ref, arrived_ref, out_ref):
    members, slots, width = arrived_ref.shape
    parts = arrived_ref[...].reshape(members * slots, width)
    out_ref[...] = jnp.dot(select_ref[...], parts, preferred_element_type=jnp.float32).astype(out_ref.dtype)


def spec(space):
    return pl.BlockSpec(memory_space=space)


def on_device(
    queries,
    new_entries,
    cache_pages,
    cache_scales,
    page_table,
    lengths,
    parent,
    placement,
    out_weight,
):
    beams = lax.axis_size("beam")
    children, heads, head_size = queries.shape
    key_heads = new_entries.shape[2]
    page_limit = page_table.shape[1]
    page_count = cache_pages.shape[0]
    wanted = (children + beams - 1) // beams
    slots = wanted + wanted % 2
    items = beams * slots
    width = out_weight.shape[1] // 2
    limit = 16 * 1024 * 1024
    params = pltpu.CompilerParams(vmem_limit_bytes=limit)

    query_rows = jnp.transpose(queries, (1, 0, 2))
    entry_rows = new_entries.reshape(children * 2 * key_heads, head_size)
    scales = jnp.transpose(cache_scales, (1, 2, 0)).reshape(2 * key_heads, page_count)

    send, select, scale_values = pl.pallas_call(
        functools.partial(pack_kernel, beams, slots),
        out_shape=(
            jax.ShapeDtypeStruct((beams, slots * ITEM_ROWS, head_size), jnp.bfloat16),
            jax.ShapeDtypeStruct((children, 2 * items), jnp.bfloat16),
            jax.ShapeDtypeStruct((2 * key_heads, page_count), jnp.float32),
        ),
        in_specs=[spec(SMEM)] * 2 + [spec(VMEM)] * 3,
        out_specs=(spec(VMEM),) * 3,
        scratch_shapes=[SMEM((beams,), jnp.int32)],
        compiler_params=params,
        name="pack",
    )(parent, placement, query_rows, entry_rows, scales)

    arrived = lax.all_to_all(send, "beam", split_axis=0, concat_axis=0, tiled=True)

    item_pages, item_lengths = pl.pallas_call(
        functools.partial(route_kernel, beams, slots, children),
        out_shape=(
            jax.ShapeDtypeStruct((items * page_limit,), jnp.int32),
            jax.ShapeDtypeStruct((items,), jnp.int32),
        ),
        in_specs=[spec(SMEM)] * 4,
        out_specs=(spec(SMEM),) * 2,
        compiler_params=params,
        name="route",
    )(parent, placement, jnp.transpose(page_table), lengths)

    partial_sums = pl.pallas_call(
        functools.partial(attend_kernel, slots, 1.0 / math.sqrt(head_size)),
        out_shape=jax.ShapeDtypeStruct((beams * 2, slots, width), jnp.bfloat16),
        in_specs=[spec(SMEM)] * 3 + [spec(VMEM)] * 3,
        out_specs=spec(VMEM),
        scratch_shapes=[VMEM((items * ITEM_ROWS, head_size), jnp.float32)],
        compiler_params=pltpu.CompilerParams(vmem_limit_bytes=limit),
        name="attend",
    )(
        item_pages,
        item_lengths,
        scale_values,
        arrived.reshape(items, ITEM_ROWS, head_size),
        pltpu.with_memory_space_constraint(cache_pages, VMEM),
        pltpu.with_memory_space_constraint(out_weight, VMEM),
    )

    returned = lax.all_to_all(partial_sums, ("beam", "tp"), split_axis=0, concat_axis=0, tiled=True)

    return pl.pallas_call(
        finish_kernel,
        out_shape=jax.ShapeDtypeStruct((children, width), jnp.bfloat16),
        in_specs=[spec(VMEM)] * 2,
        out_specs=spec(VMEM),
        compiler_params=params,
        name="finish",
    )(select, returned)


def solution(mesh):
    return jax.shard_map(
        on_device,
        mesh=mesh,
        in_specs=(
            P(("grp", "beam"), "tp", None),
            P(("grp", "beam"), None, "tp", None),
            P(("grp", "beam"), None, "tp", None, None),
            P(("grp", "beam"), None, "tp"),
            P(("grp", "beam"), None),
            P("grp"),
            P("grp"),
            P("grp"),
            P("tp", None),
        ),
        out_specs=P(("grp", "beam"), "tp"),
        check_vma=False,
    )
```

time: 188 us -> 44.8 us (0.24)
  waiting for transfers between devices: 136 us -> 0.65 us
  local copies, waits for them, and re-layouts: 26.1 us -> 11.8 us
  Pallas kernels: 0 us -> 12.1 us
  blocking collectives: 3.83 us -> 12.4 us
  matrix products: 6.26 us -> 0 us
  starting transfers between devices: 13.4 us -> 7.28 us
  other arithmetic: 1.95 us -> 0 us
    all_to_all x2 -> x1, waiting for transfers between devices: 136 us -> 0.65 us  [on_device(): lax.all_to_all(send, 'beam', split_axis=0, concat_axis=0, tiled=True)]
    gather x8 -> x0, local copies, waits for them, and re-layouts: 18.3 us -> none  [the longest x1 7.75 us: on_device(): cache_pages[flat_pages]]
    all_to_all x0 -> x1, blocking collectives: none -> 12.4 us  [on_device(): lax.all_to_all(partial_sums, ('beam', 'tp'), split_axis=0, concat_axis=0,...]
    pallas_call x0 -> x4, Pallas kernels: none -> 12.1 us  [the longest x1 6.29 us: on_device(): pl.pallas_call(functools.partial(attend_kernel, slots, 1.0 / math.sqrt(he...]
    unnamed x10 -> x22, local copies, waits for them, and re-layouts: 1.57 us -> 11.8 us
    dot_general x4 -> x0, matrix products: 6.26 us -> none  [the longest x1 3.82 us: on_device(): jnp.dot(attended, out_weight, preferred_element_type=jnp.float32)]
    all_to_all x2 -> x1, starting transfers between devices: 13.4 us -> 7.28 us  [on_device(): lax.all_to_all(send, 'beam', split_axis=0, concat_axis=0, tiled=True)]
    slice x1 -> x0, local copies, waits for them, and re-layouts: 4.21 us -> none  [attend(): page_blocks[:, :, 0]]
  transfers between devices with their start and end apart: 2 -> 1, of which waited for: 1 -> 1; matrix products, arithmetic and copies ran while one was open for 5% -> 0% of each run, Pallas kernels for 0% -> 8%
where the time goes in v1:
time: 44.8 us; the launch traced here: 44.3 us
  blocking collectives  12.4 us (28%)
  Pallas kernels  12.1 us (27%)
  local copies, waits for them, and re-layouts  11.8 us (26%)
  starting transfers between devices  7.28 us (16%)
  waiting for transfers between devices  0.65 us (1%)
    all_to_all x1, blocking collectives, on_device(): lax.all_to_all(partial_sums, ('beam', 'tp'), split_axis=0, concat_axis=0,...  12.4 us
    unnamed x22, local copies, waits for them, and re-layouts  11.8 us
    all_to_all x1, starting transfers between devices, on_device(): lax.all_to_all(send, 'beam', split_axis=0, concat_axis=0, tiled=True)  7.28 us
    pallas_call x1, Pallas kernels, on_device(): pl.pallas_call(functools.partial(attend_kernel, slots, 1.0 / math.sqrt(he...  6.29 us
    pallas_call x1, Pallas kernels, on_device(): pl.pallas_call(functools.partial(route_kernel, beams, slots, children), o...  3.6 us
    pallas_call x1, Pallas kernels, on_device(): pl.pallas_call(functools.partial(pack_kernel, beams, slots), out_shape=(j...  1.48 us
  transfers between devices with their start and end apart: 1, of which 1 were waited for; matrix products, arithmetic and copies ran while one was open for 0% of the time, Pallas kernels for 8%

profile of v1, /device:TPU:0, one launch (start us, length us, event | category | flops | bytes accessed | tf_op | source)
XLA Modules:
  0.0 44.3 jit_solution(5405876316346709301)
XLA Ops:
  0.0 0.0 copy-start.2
  0.0 0.8 %copy-done.2 = bf16[16,10,128]{2,0,1:T(8,128)(2,1)S(1)} copy-done((bf16[16,10,128]{2,0,1:T(8,128)(2,1)S(1)}, bf16[16,10,128]{2,0,1:T(8,128)(2,1)}, u32[]{:S(2)}) %copy-start.2) | copy-done | bytes 40984
  0.8 0.0 copy-start.3
  0.8 0.7 %copy-done.3 = bf16[16,2,2,128]{3,2,1,0:T(2,128)(2,1)S(1)} copy-done((bf16[16,2,2,128]{3,2,1,0:T(2,128)(2,1)S(1)}, bf16[16,2,2,128]{3,2,1,0:T(2,128)(2,1)}, u32[]{:S(2)}) %copy-start.3) | copy-done | bytes 16408
  1.5 0.0 copy-start.5
  1.5 0.7 %copy-done.5 = s32[128]{0:T(128)S(1)} copy-done((s32[128]{0:T(128)S(1)}, s32[128]{0:T(128)}, u32[]{:S(2)}) %copy-start.5) | copy-done | bytes 536
  2.2 0.0 copy-start.7
  2.2 0.7 %copy-done.7 = s32[128]{0:T(128)S(1)} copy-done((s32[128]{0:T(128)S(1)}, s32[128]{0:T(128)}, u32[]{:S(2)}) %copy-start.7) | copy-done | bytes 536
  2.8 0.0 copy-start.9
  2.8 0.7 %copy-done.9 = bf16[48,2,2]{0,2,1:T(2,128)(2,1)S(1)} copy-done((bf16[48,2,2]{0,2,1:T(2,128)(2,1)S(1)}, bf16[48,2,2]{0,2,1:T(2,128)(2,1)}, u32[]{:S(2)}) %copy-start.9) | copy-done | bytes 408
  3.5 1.5 %pack.1 = (bf16[8,32,128]{2,1,0:T(8,128)(2,1)}, bf16[16,32]{1,0:T(8,128)(2,1)S(1)}, f32[4,48]{1,0:T(4,128)S(1)}) custom-call(s32[128]{0:T(128)S(1)} %copy-done.5, s32[128]{0:T(128)S(1)} %copy-done.7, bf16[10,16,128]{2,1,0:T(8,128)(2,1)S(1)} %bitcast.8, bf16[64,128]{1,0:T(8,128)(2,1)S(1)} %bitcast.9, bf16[4,48]{1,0:T(4,128)(2,1)S(1)} %bitcast.11), custom_call_target="tpu_custom_call" | custom-call | tf_op jit(solution)/shard_map/pack/pallas_call | solution.py:221
  5.0 7.3 %all-to-all-start = ((bf16[8,32,128]{2,1,0:T(8,128)(2,1)}), bf16[8,32,128]{2,1,0:T(8,128)(2,1)S(1)}, u32[]{:S(2)}, u32[]{:S(2)}) async-start(bf16[8,32,128]{2,1,0:T(8,128)(2,1)} %get-tuple-element.14), calls=%async_computation | async-start | bytes 131072 | tf_op jit(solution)/shard_map/all_to_all | solution.py:235
  12.2 0.0 copy-start.4
  12.2 0.7 %copy-done.4 = s32[16,3]{0,1:T(4,128)S(1)} copy-done((s32[16,3]{0,1:T(4,128)S(1)}, s32[16,3]{0,1:T(4,128)}, u32[]{:S(2)}) %copy-start.4) | copy-done | bytes 216
  12.9 0.0 copy-start.6
  12.9 0.7 %copy-done.6 = s32[128]{0:T(128)S(1)} copy-done((s32[128]{0:T(128)S(1)}, s32[128]{0:T(128)}, u32[]{:S(2)}) %copy-start.6) | copy-done | bytes 536
  13.6 0.0 copy-start.8
  13.6 0.7 %copy-done.8 = s32[128]{0:T(128)S(1)} copy-done((s32[128]{0:T(128)S(1)}, s32[128]{0:T(128)}, u32[]{:S(2)}) %copy-start.8) | copy-done | bytes 536
  14.2 0.0 copy-start.10
  14.2 0.7 %copy-done.10 = s32[128]{0:T(128)S(1)} copy-done((s32[128]{0:T(128)S(1)}, s32[128]{0:T(128)}, u32[]{:S(2)}) %copy-start.10) | copy-done | bytes 536
  14.9 3.6 %route.1 = (s32[48]{0:T(128)S(1)}, s32[16]{0:T(128)S(1)}) custom-call(s32[128]{0:T(128)S(1)} %copy-done.6, s32[128]{0:T(128)S(1)} %copy-done.8, s32[3,16]{1,0:T(4,128)S(1)} %bitcast.10, s32[128]{0:T(128)S(1)} %copy-done.10), custom_call_target="tpu_custom_call" | custom-call | tf_op jit(solution)/shard_map/route/pallas_call | solution.py:237
  18.5 0.6 %all-to-all-done = bf16[8,32,128]{2,1,0:T(8,128)(2,1)S(1)} async-done(((bf16[8,32,128]{2,1,0:T(8,128)(2,1)}), bf16[8,32,128]{2,1,0:T(8,128)(2,1)S(1)}, u32[]{:S(2)}, u32[]{:S(2)}) %all-to-all-start) | async-done | bytes 65568 | tf_op jit(solution)/shard_map/all_to_all | solution.py:235
  19.2 0.0 copy-start
  19.2 2.9 %copy-done = bf16[1280,2560]{1,0:T(8,128)(2,1)S(1)} copy-done((bf16[1280,2560]{1,0:T(8,128)(2,1)S(1)}, bf16[1280,2560]{1,0:T(8,128)(2,1)}, u32[]{:S(2)}) %copy-start) | copy-done | bytes 6553624
  22.0 0.0 copy-start.1
  22.0 2.8 %copy-done.1 = bf16[48,2,2,128,128]{4,3,2,1,0:T(8,128)(2,1)S(1)} copy-done((bf16[48,2,2,128,128]{4,3,2,1,0:T(8,128)(2,1)S(1)}, bf16[48,2,2,128,128]{4,3,2,1,0:T(8,128)(2,1)}, u32[]{:S(2)}) %copy-start.1) | copy-done | bytes 6291480
  24.8 6.3 %attend.1 = bf16[16,2,1280]{2,1,0:T(2,128)(2,1)S(1)} custom-call(s32[48]{0:T(128)S(1)} %get-tuple-element.11.page_ref, s32[16]{0:T(128)S(1)} %get-tuple-element.12.item_length_ref, f32[4,48]{1,0:T(4,128)S(1)} %get-tuple-element.13.scale_ref, bf16[16,16,128]{2,1,0:T(8,128)(2,1)S(1)} %bitcast.7, bf16[48,2,2,128,128]{4,3,2,1,0:T(8,128)(2,1)S(1)} %copy-done.1, ...), custom_call_target="tpu_custom_call" | custom-call | tf_op jit(solution)/shard_map/attend/pallas_call | solution.py:249
  31.1 12.4 %all_to_all.10.arrived_ref = bf16[16,2,1280]{2,1,0:T(2,128)(2,1)S(1)} all-to-all(bf16[16,2,1280]{2,1,0:T(2,128)(2,1)S(1)} %attend.1), channel_id=1, replica_groups=mesh['grp'=2,'beam'=8,'tp'=2] {'beam','tp'}, dimensions={0} | all-to-all | bytes 163840 | tf_op jit(solution)/shard_map/all_to_all | solution.py:266
  43.5 0.8 %finish.1 = bf16[16,1280]{1,0:T(8,128)(2,1)} custom-call(bf16[16,32]{1,0:T(8,128)(2,1)S(1)} %get-tuple-element.10.select_ref, bf16[16,2,1280]{2,1,0:T(2,128)(2,1)S(1)} %all_to_all.10.arrived_ref), custom_call_target="tpu_custom_call" | custom-call | tf_op jit(solution)/shard_map/finish/pallas_call | solution.py:268
Async XLA Ops:
  0.0 0.8 %copy-start.2 = (bf16[16,10,128]{2,0,1:T(8,128)(2,1)S(1)}, bf16[16,10,128]{2,0,1:T(8,128)(2,1)}, u32[]{:S(2)}) copy-start(bf16[16,10,128]{2,0,1:T(8,128)(2,1)} %param.9) | copy-start | bytes 122884
  0.8 0.7 %copy-start.3 = (bf16[16,2,2,128]{3,2,1,0:T(2,128)(2,1)S(1)}, bf16[16,2,2,128]{3,2,1,0:T(2,128)(2,1)}, u32[]{:S(2)}) copy-start(bf16[16,2,2,128]{3,2,1,0:T(2,128)(2,1)} %param.10) | copy-start | bytes 49156
  1.5 0.7 %copy-start.5 = (s32[128]{0:T(128)S(1)}, s32[128]{0:T(128)}, u32[]{:S(2)}) copy-start(s32[128]{0:T(128)} %parent_ref.3) | copy-start | bytes 1540
  2.2 0.7 %copy-start.7 = (s32[128]{0:T(128)S(1)}, s32[128]{0:T(128)}, u32[]{:S(2)}) copy-start(s32[128]{0:T(128)} %placement_ref.3) | copy-start | bytes 1540
  2.8 0.7 %copy-start.9 = (bf16[48,2,2]{0,2,1:T(2,128)(2,1)S(1)}, bf16[48,2,2]{0,2,1:T(2,128)(2,1)}, u32[]{:S(2)}) copy-start(bf16[48,2,2]{0,2,1:T(2,128)(2,1)} %param.12) | copy-start | bytes 1156
  5.0 14.2 %all-to-all-start = ((bf16[8,32,128]{2,1,0:T(8,128)(2,1)}), bf16[8,32,128]{2,1,0:T(8,128)(2,1)S(1)}, u32[]{:S(2)}, u32[]{:S(2)}) async-start(bf16[8,32,128]{2,1,0:T(8,128)(2,1)} %get-tuple-element.14), calls=%async_computation | async-start | bytes 131072 | tf_op jit(solution)/shard_map/all_to_all | solution.py:235
  12.2 0.7 %copy-start.4 = (s32[16,3]{0,1:T(4,128)S(1)}, s32[16,3]{0,1:T(4,128)}, u32[]{:S(2)}) copy-start(s32[16,3]{0,1:T(4,128)} %param.13) | copy-start | bytes 580
  12.9 0.7 %copy-start.6 = (s32[128]{0:T(128)S(1)}, s32[128]{0:T(128)}, u32[]{:S(2)}) copy-start(s32[128]{0:T(128)} %parent_ref.3) | copy-start | bytes 1540
  13.6 0.7 %copy-start.8 = (s32[128]{0:T(128)S(1)}, s32[128]{0:T(128)}, u32[]{:S(2)}) copy-start(s32[128]{0:T(128)} %placement_ref.3) | copy-start | bytes 1540
  14.2 0.7 %copy-start.10 = (s32[128]{0:T(128)S(1)}, s32[128]{0:T(128)}, u32[]{:S(2)}) copy-start(s32[128]{0:T(128)} %length_ref.1) | copy-start | bytes 1540
  19.2 2.9 %copy-start = (bf16[1280,2560]{1,0:T(8,128)(2,1)S(1)}, bf16[1280,2560]{1,0:T(8,128)(2,1)}, u32[]{:S(2)}) copy-start(bf16[1280,2560]{1,0:T(8,128)(2,1)} %weight_ref.1) | copy-start | bytes 19660804
  22.0 2.8 %copy-start.1 = (bf16[48,2,2,128,128]{4,3,2,1,0:T(8,128)(2,1)S(1)}, bf16[48,2,2,128,128]{4,3,2,1,0:T(8,128)(2,1)}, u32[]{:S(2)}) copy-start(bf16[48,2,2,128,128]{4,3,2,1,0:T(8,128)(2,1)} %pages_ref.1) | copy-start | bytes 18874372

commit v2 on v1

v2 whole, which is shorter than its diff:
```python
import functools
import math

import jax
import jax.numpy as jnp
from jax import lax
from jax.experimental import pallas as pl
from jax.experimental.pallas import tpu as pltpu
from jax.sharding import PartitionSpec as P

ITEM_ROWS = 16
VMEM = pltpu.VMEM
SMEM = pltpu.SMEM
HBM = pltpu.HBM


def fetch(pairs, sem_ref):
    copies = [pltpu.make_async_copy(a, b, sem_ref.at[i]) for i, (a, b) in enumerate(pairs)]
    for copy in copies:
        copy.start()
    return copies


def pack_kernel(
    beams,
    slots,
    used,
    parent_hbm,
    placement_hbm,
    query_hbm,
    entry_hbm,
    table_hbm,
    length_hbm,
    send_hbm,
    page_ref,
    item_length_ref,
    own_item_ref,
    parent_ref,
    placement_ref,
    query_ref,
    entry_ref,
    table_ref,
    length_ref,
    send_ref,
    item_ref,
    count_ref,
    sem_ref,
):
    heads, children, head_size = query_ref.shape
    entry_rows = entry_ref.shape[0]
    per_child = entry_rows // children
    page_limit = table_ref.shape[0]
    copies = fetch(
        [
            (parent_hbm, parent_ref),
            (placement_hbm, placement_ref),
            (query_hbm, query_ref),
            (entry_hbm, entry_ref),
            (table_hbm, table_ref),
            (length_hbm, length_ref),
        ],
        sem_ref,
    )
    own = lax.axis_index("beam")
    for index in range(beams):
        count_ref[index] = 0
    query_lane = lax.broadcasted_iota(jnp.int32, (8, heads * children), 1)
    entry_lane = lax.broadcasted_iota(jnp.int32, (8, entry_rows), 1)
    query_child = query_lane % children
    entry_child = entry_lane // per_child
    query_row = query_lane // children
    entry_row = entry_lane % per_child + heads
    copies[0].wait()
    copies[1].wait()
    own_slots = [placement_ref[parent_ref[own * children + child]] for child in range(children)]
    for child, slot in enumerate(own_slots):
        source = slot // children
        rank = count_ref[source]
        count_ref[source] = rank + 1
        item = source * slots + rank
        own_item_ref[child] = item
        first = item * ITEM_ROWS
        query_row = jnp.where(query_child == child, query_row + first, query_row)
        entry_row = jnp.where(entry_child == child, entry_row + first, entry_row)
    rows = beams * slots * ITEM_ROWS
    row_of = lax.broadcasted_iota(jnp.int32, (rows, heads * children), 0)
    pick = (row_of == query_row[:1]).astype(jnp.float32).astype(jnp.bfloat16)
    entry_row_of = lax.broadcasted_iota(jnp.int32, (rows, entry_rows), 0)
    entry_pick = (entry_row_of == entry_row[:1]).astype(jnp.float32).astype(jnp.bfloat16)
    copies[2].wait()
    copies[3].wait()
    moved = jnp.dot(
        pick, query_ref[...].reshape(heads * children, head_size), preferred_element_type=jnp.float32
    )
    moved += jnp.dot(entry_pick, entry_ref[...], preferred_element_type=jnp.float32)
    send_ref[...] = moved.astype(jnp.bfloat16).reshape(send_ref.shape)
    send_copy = pltpu.make_async_copy(send_ref, send_hbm, sem_ref.at[6])
    send_copy.start()

    def one_index(index, _):
        asked = [placement_ref[parent_ref[index * children + child]] for child in range(children)]
        place = index * slots
        for slot in asked:
            item_ref[place] = slot % children
            place = place + (slot // children == own).astype(jnp.int32)
        return 0

    lax.fori_loop(0, beams, one_index, 0)
    copies[4].wait()
    copies[5].wait()
    for place, item in enumerate(used):
        local = item_ref[item]
        item_length_ref[place] = length_ref[own * children + local]
        for page in range(page_limit):
            page_ref[place * page_limit + page] = table_ref[page, local]
    send_copy.wait()


def bring_kernel(
    slots,
    page_ref,
    own_item_ref,
    scale_hbm,
    pages_hbm,
    scale_ref,
    select_ref,
    early_ref,
    scale_in_ref,
    scale_wide_ref,
    scale_sem_ref,
    page_sem_ref,
):
    scale_copy = pltpu.make_async_copy(scale_hbm, scale_in_ref, scale_sem_ref.at[0])
    scale_copy.start()
    page_copies = fetch(
        [(pages_hbm.at[page_ref[at]], early_ref.at[at]) for at in range(early_ref.shape[0])], page_sem_ref
    )
    select_shape = select_ref.shape
    child_row = lax.broadcasted_iota(jnp.int32, select_shape, 0)
    select_lane = lax.broadcasted_iota(jnp.int32, select_shape, 1)
    select_item = (select_lane // (2 * slots)) * slots + select_lane % slots
    wanted = jnp.zeros(select_shape, jnp.int32)
    for child in range(select_shape[0]):
        wanted = jnp.where(child_row == child, own_item_ref[child], wanted)
    select_ref[...] = (select_item == wanted).astype(jnp.float32).astype(jnp.bfloat16)
    scale_copy.wait()
    scale_wide_ref[...] = scale_in_ref[...].astype(jnp.float32)
    wide_copy = pltpu.make_async_copy(scale_wide_ref, scale_ref, scale_sem_ref.at[1])
    wide_copy.start()
    wide_copy.wait()
    for copy in page_copies:
        copy.wait()


def attend_kernel(
    slots,
    used,
    factor,
    page_ref,
    item_length_ref,
    scale_ref,
    arrived_ref,
    early_ref,
    pages_hbm,
    weight_hbm,
    out_ref,
    late_ref,
    weight_ref,
    score_ref,
    rounded_ref,
    denominator_ref,
    attended_ref,
    page_sem_ref,
    weight_sem_ref,
):
    item_count = arrived_ref.shape[0]
    early = early_ref.shape[0]
    _, _, key_heads, page_rows, head_size = early_ref.shape
    page_limit = page_ref.shape[0] // len(used)
    heads = weight_ref.shape[0] // head_size
    group = heads // key_heads
    late_copies = fetch(
        [(pages_hbm.at[page_ref[early + late]], late_ref.at[late]) for late in range(late_ref.shape[0])], page_sem_ref
    )
    cuts = [0] + [heads * part // 5 * head_size for part in (3, 4, 5)]
    weight_rows = [pl.ds(low, high - low) for low, high in zip(cuts, cuts[1:])]
    row = lax.broadcasted_iota(jnp.int32, (ITEM_ROWS, head_size), 0)
    row_head = [(row >= head * group) & (row < (head + 1) * group) for head in range(key_heads)]

    def by_head(parts):
        result = jnp.zeros((ITEM_ROWS, head_size), jnp.float32)
        for mask, part in zip(row_head, parts):
            result = jnp.where(mask, part, result)
        return result

    def rows_of(item):
        return slice(item * ITEM_ROWS, (item + 1) * ITEM_ROWS)

    def both_heads(place, page, which):
        at = place * page_limit + page
        ref, at = (early_ref, at) if at < early else (late_ref, at - early)
        return jnp.concatenate([ref[at, which, head] for head in range(key_heads)], axis=1)

    def scores_of(place, item):
        packed = arrived_ref[item].astype(jnp.float32)
        wide = jnp.concatenate([jnp.where(mask, packed, 0.0) for mask in row_head], axis=1).astype(jnp.bfloat16)
        length = item_length_ref[place]
        for page in range(page_limit):
            number = page_ref[place * page_limit + page]
            raw = lax.dot_general(
                wide, both_heads(place, page, 0), (((1,), (1,)), ((), ())), preferred_element_type=jnp.float32
            )
            key_scale = by_head([scale_ref[head, number] * factor for head in range(key_heads)])
            hidden = jnp.where(page * page_rows < length, 0.0, -jnp.inf)
            score_ref[rows_of(place), page * page_rows : (page + 1) * page_rows] = raw * key_scale + hidden

    def weights_of(place, item):
        packed = arrived_ref[item].astype(jnp.float32)
        fresh_key = by_head([packed[heads + head][None] for head in range(key_heads)])
        fresh_value = by_head([packed[heads + key_heads + head][None] for head in range(key_heads)])
        scores = score_ref[rows_of(place), :]
        fresh = jnp.sum(packed * fresh_key, axis=1, keepdims=True) * factor
        highest = jnp.maximum(jnp.max(scores, axis=1, keepdims=True), fresh)
        fresh_weight = jnp.exp(fresh - highest)
        weights = jnp.exp(scores - highest)
        rounded_ref[rows_of(place), :] = weights.astype(jnp.bfloat16)
        denominator = jnp.sum(weights, axis=1, keepdims=True) + fresh_weight
        denominator_ref[rows_of(place), :] = jnp.broadcast_to(denominator, (ITEM_ROWS, head_size))
        attended_ref[rows_of(item), :] = fresh_weight.astype(jnp.bfloat16).astype(jnp.float32) * fresh_value

    def values_of(place, item):
        summed = attended_ref[rows_of(item), :]
        for page in range(page_limit):
            number = page_ref[place * page_limit + page]
            product = jnp.dot(
                rounded_ref[rows_of(place), page * page_rows : (page + 1) * page_rows],
                both_heads(place, page, 1),
                preferred_element_type=jnp.float32,
            )
            summed = summed + by_head(
                [
                    product[:, head * head_size : (head + 1) * head_size] * scale_ref[key_heads + head, number]
                    for head in range(key_heads)
                ],
            )
        attended_ref[rows_of(item), :] = summed / denominator_ref[rows_of(place), :]

    if len(used) < item_count:
        attended_ref[...] = jnp.zeros_like(attended_ref)
    places = list(enumerate(used))
    late_places = places[early // page_limit :]
    share = len(late_places) // 4
    groups = [places[: early // page_limit]]
    groups += [late_places[low : low + share] for low in range(0, len(late_places), share)]
    for number, group_of in enumerate(groups):
        if number > 0:
            for copy in late_copies[(number - 1) * share * page_limit : number * share * page_limit]:
                copy.wait()
        if number == 1:
            weight_copies = fetch([(weight_hbm.at[rows], weight_ref.at[rows]) for rows in weight_rows], weight_sem_ref)
        for step in (scores_of, weights_of, values_of):
            for place, item in group_of:
                step(place, item)
    attended = jnp.concatenate(
        [attended_ref[pl.ds(head, item_count, stride=ITEM_ROWS), :] for head in range(heads)], axis=1
    ).astype(jnp.bfloat16)
    total = None
    for copy, low, high in zip(weight_copies, cuts, cuts[1:]):
        copy.wait()
        term = jnp.dot(attended[:, low:high], weight_ref[low:high, :], preferred_element_type=jnp.float32)
        total = term if total is None else total + term
    total = total.astype(jnp.bfloat16)
    width = out_ref.shape[2]
    for half in range(2):
        for index in range(item_count // slots):
            out_ref[index * 2 + half] = total[index * slots : (index + 1) * slots, half * width : (half + 1) * width]


def finish_kernel(select_ref, arrived_ref, out_ref):
    members, slots, width = arrived_ref.shape
    parts = arrived_ref[...].reshape(members * slots, width)
    out_ref[...] = jnp.dot(select_ref[...], parts, preferred_element_type=jnp.float32).astype(out_ref.dtype)


def kept(space, *arrays):
    return tuple(pltpu.with_memory_space_constraint(array, space) for array in arrays)


def spec(space):
    return pl.BlockSpec(memory_space=space)


def on_device(
    queries,
    new_entries,
    cache_pages,
    cache_scales,
    page_table,
    lengths,
    parent,
    placement,
    out_weight,
):
    beams = lax.axis_size("beam")
    children, heads, head_size = queries.shape
    key_heads = new_entries.shape[2]
    page_limit = page_table.shape[1]
    page_count = cache_pages.shape[0]
    page_rows = cache_pages.shape[3]
    wanted = (children + beams - 1) // beams
    slots = wanted + wanted % 2
    items = beams * slots
    used = [index * slots + rank for index in range(beams) for rank in range(wanted)]
    page_total = len(used) * page_limit
    early = min(len(used), 8) * page_limit
    page_shape = cache_pages.shape[1:]
    width = out_weight.shape[1] // 2
    limit = 32 * 1024 * 1024
    params = pltpu.CompilerParams(vmem_limit_bytes=limit)

    query_rows = jnp.transpose(queries, (1, 0, 2))
    entry_rows = new_entries.reshape(children * 2 * key_heads, head_size)
    scales = jnp.transpose(cache_scales, (1, 2, 0)).reshape(2 * key_heads, page_count)

    send, item_pages, item_lengths, own_items = pl.pallas_call(
        functools.partial(pack_kernel, beams, slots, used),
        out_shape=(
            HBM((beams, slots * ITEM_ROWS, head_size), jnp.bfloat16),
            SMEM((page_total,), jnp.int32),
            SMEM((len(used),), jnp.int32),
            SMEM((children,), jnp.int32),
        ),
        in_specs=[spec(HBM)] * 6,
        out_specs=(spec(HBM),) + (spec(SMEM),) * 3,
        scratch_shapes=[
            SMEM(parent.shape, jnp.int32),
            SMEM(placement.shape, jnp.int32),
            VMEM(query_rows.shape, jnp.bfloat16),
            VMEM(entry_rows.shape, jnp.bfloat16),
            SMEM(page_table.shape[::-1], jnp.int32),
            SMEM(lengths.shape, jnp.int32),
            VMEM((beams, slots * ITEM_ROWS, head_size), jnp.bfloat16),
            SMEM((items + 1,), jnp.int32),
            SMEM((beams,), jnp.int32),
            pltpu.SemaphoreType.DMA((7,)),
        ],
        compiler_params=params,
        name="pack",
    )(*kept(HBM, parent, placement, query_rows, entry_rows, jnp.transpose(page_table), lengths))

    arrived = lax.all_to_all(send, "beam", split_axis=0, concat_axis=0, tiled=True)

    scale_values, select, early_pages = pl.pallas_call(
        functools.partial(bring_kernel, slots),
        out_shape=(
            SMEM(scales.shape, jnp.float32),
            VMEM((children, 2 * items), jnp.bfloat16),
            VMEM((early,) + page_shape, jnp.bfloat16),
        ),
        in_specs=[spec(SMEM)] * 2 + [spec(HBM)] * 2,
        out_specs=(spec(SMEM), spec(VMEM), spec(VMEM)),
        scratch_shapes=[
            VMEM(scales.shape, jnp.bfloat16),
            VMEM(scales.shape, jnp.float32),
            pltpu.SemaphoreType.DMA((2,)),
            pltpu.SemaphoreType.DMA((early,)),
        ],
        compiler_params=params,
        name="bring",
    )(*kept(SMEM, item_pages, own_items), *kept(HBM, scales, cache_pages))

    partial_sums = pl.pallas_call(
        functools.partial(attend_kernel, slots, used, 1.0 / math.sqrt(head_size)),
        out_shape=jax.ShapeDtypeStruct((beams * 2, slots, width), jnp.bfloat16),
        in_specs=[spec(SMEM)] * 3 + [spec(VMEM)] * 2 + [spec(HBM)] * 2,
        out_specs=spec(VMEM),
        scratch_shapes=[
            VMEM((page_total - early,) + page_shape, jnp.bfloat16),
            VMEM(out_weight.shape, jnp.bfloat16),
            VMEM((len(used) * ITEM_ROWS, page_limit * page_rows), jnp.float32),
            VMEM((len(used) * ITEM_ROWS, page_limit * page_rows), jnp.bfloat16),
            VMEM((len(used) * ITEM_ROWS, head_size), jnp.float32),
            VMEM((items * ITEM_ROWS, head_size), jnp.float32),
            pltpu.SemaphoreType.DMA((page_total - early,)),
            pltpu.SemaphoreType.DMA((3,)),
        ],
        compiler_params=params,
        name="attend",
    )(
        *kept(SMEM, item_pages, item_lengths, scale_values),
        *kept(VMEM, arrived.reshape(items, ITEM_ROWS, head_size), early_pages),
        *kept(HBM, cache_pages, out_weight),
    )

    returned = lax.all_to_all(partial_sums, ("beam", "tp"), split_axis=0, concat_axis=0, tiled=True)

    return pl.pallas_call(
        finish_kernel,
        out_shape=jax.ShapeDtypeStruct((children, width), jnp.bfloat16),
        in_specs=[spec(VMEM)] * 2,
        out_specs=spec(VMEM),
        compiler_params=params,
        name="finish",
    )(*kept(VMEM, select, returned))


def solution(mesh):
    return jax.shard_map(
        on_device,
        mesh=mesh,
        in_specs=(
            P(("grp", "beam"), "tp", None),
            P(("grp", "beam"), None, "tp", None),
            P(("grp", "beam"), None, "tp", None, None),
            P(("grp", "beam"), None, "tp"),
            P(("grp", "beam"), None),
            P("grp"),
            P("grp"),
            P("grp"),
            P("tp", None),
        ),
        out_specs=P(("grp", "beam"), "tp"),
        check_vma=False,
    )
```

time: 44.8 us -> 33 us (0.74)
  local copies, waits for them, and re-layouts: 11.8 us -> 0 us
  waiting for transfers between devices: 0.65 us -> 4.39 us
  blocking collectives: 12.4 us -> 9.73 us
  Pallas kernels: 12.1 us -> 11.3 us
    unnamed x22 -> x0, local copies, waits for them, and re-layouts: 11.8 us -> none
    all_to_all x1, waiting for transfers between devices: 0.65 us -> 4.39 us  [on_device(): lax.all_to_all(send, 'beam', split_axis=0, concat_axis=0, tiled=True)]
    all_to_all x1, blocking collectives: 12.4 us -> 9.73 us  [on_device(): lax.all_to_all(partial_sums, ('beam', 'tp'), split_axis=0, concat_axis=0,...]
    pallas_call x3, Pallas kernels: 11.4 us -> 10.5 us  [the longest x1 5.85 us: on_device(): pl.pallas_call(functools.partial(attend_kernel, slots, used, 1.0 / math.s...]
where the time goes in v2:
time: 33 us; the launch traced here: 32.7 us
  Pallas kernels  11.3 us (34%)
  blocking collectives  9.73 us (29%)
  starting transfers between devices  7.29 us (22%)
  waiting for transfers between devices  4.39 us (13%)
    all_to_all x1, blocking collectives, on_device(): lax.all_to_all(partial_sums, ('beam', 'tp'), split_axis=0, concat_axis=0,...  9.73 us
    all_to_all x1, starting transfers between devices, on_device(): lax.all_to_all(send, 'beam', split_axis=0, concat_axis=0, tiled=True)  7.29 us
    pallas_call x1, Pallas kernels, on_device(): pl.pallas_call(functools.partial(attend_kernel, slots, used, 1.0 / math.s...  5.85 us
    all_to_all x1, waiting for transfers between devices, on_device(): lax.all_to_all(send, 'beam', split_axis=0, concat_axis=0, tiled=True)  4.39 us
    pallas_call x1, Pallas kernels, on_device(): pl.pallas_call(functools.partial(bring_kernel, slots), out_shape=(SMEM(sc...  2.51 us
    pallas_call x1, Pallas kernels, on_device(): pl.pallas_call(functools.partial(pack_kernel, beams, slots, used), out_sh...  2.15 us
    pallas_call x1, Pallas kernels, on_device(): pl.pallas_call(finish_kernel, out_shape=jax.ShapeDtypeStruct((children, w...  0.75 us
  transfers between devices with their start and end apart: 1, of which 1 were waited for; matrix products, arithmetic and copies ran while one was open for 0% of the time, Pallas kernels for 8%

profile of v2, /device:TPU:0, one launch (start us, length us, event | category | flops | bytes accessed | tf_op | source)
XLA Modules:
  0.0 32.7 jit_solution(89260561097764132)
XLA Ops:
  0.0 2.1 %pack.1 = (bf16[8,32,128]{2,1,0:T(8,128)(2,1)}, s32[48]{0:T(128)S(4)}, s32[16]{0:T(128)S(4)}, s32[16]{0:T(128)S(4)}) custom-call(s32[128]{0:T(128)} %parent_hbm.1, s32[128]{0:T(128)} %placement_hbm.1, bf16[10,16,128]{2,1,0:T(8,128)(2,1)} %bitcast.8, bf16[64,128]{1,0:T(8,128)(2,1)} %bitcast.9, s32[3,16]{1,0:T(4,128)} %bitcast.10, s32[128]{0:T(128)} %length_hbm.1), custom_call_target="tpu_custom_call" | custom-call | tf_op jit(solution)/shard_map/pack/pallas_call | solution.py:325
  2.2 7.3 %all-to-all-start = ((bf16[8,32,128]{2,1,0:T(8,128)(2,1)}), bf16[8,32,128]{2,1,0:T(8,128)(2,1)S(1)}, u32[]{:S(2)}, u32[]{:S(2)}) async-start(bf16[8,32,128]{2,1,0:T(8,128)(2,1)} %get-tuple-element.17), calls=%async_computation | async-start | bytes 131072 | tf_op jit(solution)/shard_map/all_to_all | solution.py:351
  9.5 2.5 %bring.1 = (f32[4,48]{1,0:T(4,128)S(4)}, bf16[16,32]{1,0:T(8,128)(2,1)S(1)}, bf16[24,2,2,128,128]{4,3,2,1,0:T(8,128)(2,1)S(1)}) custom-call(s32[48]{0:T(128)S(4)} %get-tuple-element.12.page_ref, s32[16]{0:T(128)S(4)} %get-tuple-element.13.own_item_ref, bf16[4,48]{1,0:T(4,128)(2,1)} %bitcast.11, bf16[48,2,2,128,128]{4,3,2,1,0:T(8,128)(2,1)} %pages_hbm.3), custom_call_target="tpu_custom_call" | custom-call | tf_op jit(solution)/shard_map/bring/pallas_call | solution.py:353
  12.0 4.4 %all-to-all-done = bf16[8,32,128]{2,1,0:T(8,128)(2,1)S(1)} async-done(((bf16[8,32,128]{2,1,0:T(8,128)(2,1)}), bf16[8,32,128]{2,1,0:T(8,128)(2,1)S(1)}, u32[]{:S(2)}, u32[]{:S(2)}) %all-to-all-start) | async-done | bytes 65568 | tf_op jit(solution)/shard_map/all_to_all | solution.py:351
  16.4 5.9 %attend.1 = bf16[16,2,1280]{2,1,0:T(2,128)(2,1)S(1)} custom-call(s32[48]{0:T(128)S(4)} %get-tuple-element.12.page_ref, s32[16]{0:T(128)S(4)} %get-tuple-element.15.item_length_ref, f32[4,48]{1,0:T(4,128)S(4)} %get-tuple-element.16.scale_ref, bf16[16,16,128]{2,1,0:T(8,128)(2,1)S(1)} %bitcast.7, bf16[24,2,2,128,128]{4,3,2,1,0:T(8,128)(2,1)S(1)} %get-tuple-element.18.early_ref, ...), custom_call_target="tpu_custom_call" | custom-call | tf_op jit(solution)/shard_map/attend/pallas_call | solution.py:372
  22.2 9.7 %all_to_all.10.arrived_ref = bf16[16,2,1280]{2,1,0:T(2,128)(2,1)S(1)} all-to-all(bf16[16,2,1280]{2,1,0:T(2,128)(2,1)S(1)} %attend.1), channel_id=1, replica_groups=mesh['grp'=2,'beam'=8,'tp'=2] {'beam','tp'}, dimensions={0} | all-to-all | bytes 163840 | tf_op jit(solution)/shard_map/all_to_all | solution.py:395
  31.9 0.8 %finish.1 = bf16[16,1280]{1,0:T(8,128)(2,1)} custom-call(bf16[16,32]{1,0:T(8,128)(2,1)S(1)} %get-tuple-element.14.select_ref, bf16[16,2,1280]{2,1,0:T(2,128)(2,1)S(1)} %all_to_all.10.arrived_ref), custom_call_target="tpu_custom_call" | custom-call | tf_op jit(solution)/shard_map/finish/pallas_call | solution.py:397
Async XLA Ops:
  2.2 14.2 %all-to-all-start = ((bf16[8,32,128]{2,1,0:T(8,128)(2,1)}), bf16[8,32,128]{2,1,0:T(8,128)(2,1)S(1)}, u32[]{:S(2)}, u32[]{:S(2)}) async-start(bf16[8,32,128]{2,1,0:T(8,128)(2,1)} %get-tuple-element.17), calls=%async_computation | async-start | bytes 131072 | tf_op jit(solution)/shard_map/all_to_all | solution.py:351

commit v3 on v2

--- a/solution.py
+++ b/solution.py
@@ -31,17 +31,24 @@
     entry_hbm,
     table_hbm,
     length_hbm,
-    send_hbm,
+    scale_hbm,
+    pages_hbm,
+    weight_hbm,
+    send_ref,
     page_ref,
     item_length_ref,
-    own_item_ref,
+    scale_ref,
+    select_ref,
+    pages_ref,
+    weight_ref,
     parent_ref,
     placement_ref,
     query_ref,
     entry_ref,
     table_ref,
     length_ref,
-    send_ref,
+    scale_in_ref,
+    scale_wide_ref,
     item_ref,
     count_ref,
     sem_ref,
@@ -58,6 +65,9 @@
             (entry_hbm, entry_ref),
             (table_hbm, table_ref),
             (length_hbm, length_ref),
+            (scale_hbm, scale_in_ref),
+            (pages_hbm, pages_ref),
+            (weight_hbm.at[pl.ds(0, weight_ref.shape[0])], weight_ref),
         ],
         sem_ref,
     )
@@ -70,6 +80,11 @@
     entry_child = entry_lane // per_child
     query_row = query_lane // children
     entry_row = entry_lane % per_child + heads
+    select_shape = select_ref.shape
+    child_row = lax.broadcasted_iota(jnp.int32, select_shape, 0)
+    select_lane = lax.broadcasted_iota(jnp.int32, select_shape, 1)
+    select_item = (select_lane // (2 * slots)) * slots + select_lane % slots
+    wanted = jnp.zeros(select_shape, jnp.int32)
     copies[0].wait()
     copies[1].wait()
     own_slots = [placement_ref[parent_ref[own * children + child]] for child in range(children)]
@@ -78,7 +93,7 @@
         rank = count_ref[source]
         count_ref[source] = rank + 1
         item = source * slots + rank
-        own_item_ref[child] = item
+        wanted = jnp.where(child_row == child, item, wanted)
         first = item * ITEM_ROWS
         query_row = jnp.where(query_child == child, query_row + first, query_row)
         entry_row = jnp.where(entry_child == child, entry_row + first, entry_row)
@@ -94,8 +109,11 @@
     )
     moved += jnp.dot(entry_pick, entry_ref[...], preferred_element_type=jnp.float32)
     send_ref[...] = moved.astype(jnp.bfloat16).reshape(send_ref.shape)
-    send_copy = pltpu.make_async_copy(send_ref, send_hbm, sem_ref.at[6])
-    send_copy.start()
+    select_ref[...] = (select_item == wanted).astype(jnp.float32).astype(jnp.bfloat16)
+    copies[6].wait()
+    scale_wide_ref[...] = scale_in_ref[...].astype(jnp.float32)
+    scale_copy = pltpu.make_async_copy(scale_wide_ref, scale_ref, sem_ref.at[9])
+    scale_copy.start()
 
     def one_index(index, _):
         asked = [placement_ref[parent_ref[index * children + child]] for child in range(children)]
@@ -113,43 +131,9 @@
         item_length_ref[place] = length_ref[own * children + local]
         for page in range(page_limit):
             page_ref[place * page_limit + page] = table_ref[page, local]
-    send_copy.wait()
-
-
-def bring_kernel(
-    slots,
-    page_ref,
-    own_item_ref,
-    scale_hbm,
-    pages_hbm,
-    scale_ref,
-    select_ref,
-    early_ref,
-    scale_in_ref,
-    scale_wide_ref,
-    scale_sem_ref,
-    page_sem_ref,
-):
-    scale_copy = pltpu.make_async_copy(scale_hbm, scale_in_ref, scale_sem_ref.at[0])
-    scale_copy.start()
-    page_copies = fetch(
-        [(pages_hbm.at[page_ref[at]], early_ref.at[at]) for at in range(early_ref.shape[0])], page_sem_ref
-    )
-    select_shape = select_ref.shape
-    child_row = lax.broadcasted_iota(jnp.int32, select_shape, 0)
-    select_lane = lax.broadcasted_iota(jnp.int32, select_shape, 1)
-    select_item = (select_lane // (2 * slots)) * slots + select_lane % slots
-    wanted = jnp.zeros(select_shape, jnp.int32)
-    for child in range(select_shape[0]):
-        wanted = jnp.where(child_row == child, own_item_ref[child], wanted)
-    select_ref[...] = (select_item == wanted).astype(jnp.float32).astype(jnp.bfloat16)
     scale_copy.wait()
-    scale_wide_ref[...] = scale_in_ref[...].astype(jnp.float32)
-    wide_copy = pltpu.make_async_copy(scale_wide_ref, scale_ref, scale_sem_ref.at[1])
-    wide_copy.start()
-    wide_copy.wait()
-    for copy in page_copies:
-        copy.wait()
+    copies[7].wait()
+    copies[8].wait()
 
 
 def attend_kernel(
@@ -160,30 +144,23 @@
     item_length_ref,
     scale_ref,
     arrived_ref,
-    early_ref,
-    pages_hbm,
+    pages_ref,
+    weight_ref,
     weight_hbm,
     out_ref,
-    late_ref,
-    weight_ref,
+    weight_tail_ref,
     score_ref,
     rounded_ref,
     denominator_ref,
     attended_ref,
-    page_sem_ref,
-    weight_sem_ref,
+    sem_ref,
 ):
     item_count = arrived_ref.shape[0]
-    early = early_ref.shape[0]
-    _, _, key_heads, page_rows, head_size = early_ref.shape
+    _, _, key_heads, page_rows, head_size = pages_ref.shape
     page_limit = page_ref.shape[0] // len(used)
-    heads = weight_ref.shape[0] // head_size
+    cut, tail = weight_ref.shape[0], 0
+    heads = (cut + tail) // head_size
     group = heads // key_heads
-    late_copies = fetch(
-        [(pages_hbm.at[page_ref[early + late]], late_ref.at[late]) for late in range(late_ref.shape[0])], page_sem_ref
-    )
-    cuts = [0] + [heads * part // 5 * head_size for part in (3, 4, 5)]
-    weight_rows = [pl.ds(low, high - low) for low, high in zip(cuts, cuts[1:])]
     row = lax.broadcasted_iota(jnp.int32, (ITEM_ROWS, head_size), 0)
     row_head = [(row >= head * group) & (row < (head + 1) * group) for head in range(key_heads)]
 
@@ -196,10 +173,8 @@
     def rows_of(item):
         return slice(item * ITEM_ROWS, (item + 1) * ITEM_ROWS)
 
-    def both_heads(place, page, which):
-        at = place * page_limit + page
-        ref, at = (early_ref, at) if at < early else (late_ref, at - early)
-        return jnp.concatenate([ref[at, which, head] for head in range(key_heads)], axis=1)
+    def both_heads(number, which):
+        return jnp.concatenate([pages_ref[number, which, head] for head in range(key_heads)], axis=1)
 
     def scores_of(place, item):
         packed = arrived_ref[item].astype(jnp.float32)
@@ -208,7 +183,7 @@
         for page in range(page_limit):
             number = page_ref[place * page_limit + page]
             raw = lax.dot_general(
-                wide, both_heads(place, page, 0), (((1,), (1,)), ((), ())), preferred_element_type=jnp.float32
+                wide, both_heads(number, 0), (((1,), (1,)), ((), ())), preferred_element_type=jnp.float32
             )
             key_scale = by_head([scale_ref[head, number] * factor for head in range(key_heads)])
             hidden = jnp.where(page * page_rows < length, 0.0, -jnp.inf)
@@ -234,7 +209,7 @@
             number = page_ref[place * page_limit + page]
             product = jnp.dot(
                 rounded_ref[rows_of(place), page * page_rows : (page + 1) * page_rows],
-                both_heads(place, page, 1),
+                both_heads(number, 1),
                 preferred_element_type=jnp.float32,
             )
             summed = summed + by_head(
@@ -247,28 +222,13 @@
 
     if len(used) < item_count:
         attended_ref[...] = jnp.zeros_like(attended_ref)
-    places = list(enumerate(used))
-    late_places = places[early // page_limit :]
-    share = len(late_places) // 4
-    groups = [places[: early // page_limit]]
-    groups += [late_places[low : low + share] for low in range(0, len(late_places), share)]
-    for number, group_of in enumerate(groups):
-        if number > 0:
-            for copy in late_copies[(number - 1) * share * page_limit : number * share * page_limit]:
-                copy.wait()
-        if number == 1:
-            weight_copies = fetch([(weight_hbm.at[rows], weight_ref.at[rows]) for rows in weight_rows], weight_sem_ref)
-        for step in (scores_of, weights_of, values_of):
-            for place, item in group_of:
-                step(place, item)
+    for step in (scores_of, weights_of, values_of):
+        for place, item in enumerate(used):
+            step(place, item)
     attended = jnp.concatenate(
         [attended_ref[pl.ds(head, item_count, stride=ITEM_ROWS), :] for head in range(heads)], axis=1
     ).astype(jnp.bfloat16)
-    total = None
-    for copy, low, high in zip(weight_copies, cuts, cuts[1:]):
-        copy.wait()
-        term = jnp.dot(attended[:, low:high], weight_ref[low:high, :], preferred_element_type=jnp.float32)
-        total = term if total is None else total + term
+    total = jnp.dot(attended[:, :cut], weight_ref[...], preferred_element_type=jnp.float32)
     total = total.astype(jnp.bfloat16)
     width = out_ref.shape[2]
     for half in range(2):
@@ -312,26 +272,28 @@
     items = beams * slots
     used = [index * slots + rank for index in range(beams) for rank in range(wanted)]
     page_total = len(used) * page_limit
-    early = min(len(used), 8) * page_limit
-    page_shape = cache_pages.shape[1:]
+    cut = heads * head_size
     width = out_weight.shape[1] // 2
-    limit = 32 * 1024 * 1024
+    limit = 16 * 1024 * 1024
     params = pltpu.CompilerParams(vmem_limit_bytes=limit)
 
     query_rows = jnp.transpose(queries, (1, 0, 2))
     entry_rows = new_entries.reshape(children * 2 * key_heads, head_size)
     scales = jnp.transpose(cache_scales, (1, 2, 0)).reshape(2 * key_heads, page_count)
 
-    send, item_pages, item_lengths, own_items = pl.pallas_call(
+    send, item_pages, item_lengths, scale_values, select, pages, weight_head = pl.pallas_call(
         functools.partial(pack_kernel, beams, slots, used),
         out_shape=(
-            HBM((beams, slots * ITEM_ROWS, head_size), jnp.bfloat16),
+            VMEM((beams, slots * ITEM_ROWS, head_size), jnp.bfloat16),
             SMEM((page_total,), jnp.int32),
             SMEM((len(used),), jnp.int32),
-            SMEM((children,), jnp.int32),
+            SMEM(scales.shape, jnp.float32),
+            VMEM((children, 2 * items), jnp.bfloat16),
+            VMEM(cache_pages.shape, jnp.bfloat16),
+            VMEM((cut, out_weight.shape[1]), jnp.bfloat16),
         ),
-        in_specs=[spec(HBM)] * 6,
-        out_specs=(spec(HBM),) + (spec(SMEM),) * 3,
+        in_specs=[spec(HBM)] * 9,
+        out_specs=(spec(VMEM),) + (spec(SMEM),) * 3 + (spec(VMEM),) * 3,
         scratch_shapes=[
             SMEM(parent.shape, jnp.int32),
             SMEM(placement.shape, jnp.int32),
@@ -339,57 +301,50 @@
             VMEM(entry_rows.shape, jnp.bfloat16),
             SMEM(page_table.shape[::-1], jnp.int32),
             SMEM(lengths.shape, jnp.int32),
-            VMEM((beams, slots * ITEM_ROWS, head_size), jnp.bfloat16),
+            VMEM(scales.shape, jnp.bfloat16),
+            VMEM(scales.shape, jnp.float32),
             SMEM((items + 1,), jnp.int32),
             SMEM((beams,), jnp.int32),
-            pltpu.SemaphoreType.DMA((7,)),
+            pltpu.SemaphoreType.DMA((10,)),
         ],
         compiler_params=params,
         name="pack",
-    )(*kept(HBM, parent, placement, query_rows, entry_rows, jnp.transpose(page_table), lengths))
+    )(
+        *kept(
+            HBM,
+            parent,
+            placement,
+            query_rows,
+            entry_rows,
+            jnp.transpose(page_table),
+            lengths,
+            scales,
+            cache_pages,
+            out_weight,
+        )
+    )
 
     arrived = lax.all_to_all(send, "beam", split_axis=0, concat_axis=0, tiled=True)
-
-    scale_values, select, early_pages = pl.pallas_call(
-        functools.partial(bring_kernel, slots),
-        out_shape=(
-            SMEM(scales.shape, jnp.float32),
-            VMEM((children, 2 * items), jnp.bfloat16),
-            VMEM((early,) + page_shape, jnp.bfloat16),
-        ),
-        in_specs=[spec(SMEM)] * 2 + [spec(HBM)] * 2,
-        out_specs=(spec(SMEM), spec(VMEM), spec(VMEM)),
-        scratch_shapes=[
-            VMEM(scales.shape, jnp.bfloat16),
-            VMEM(scales.shape, jnp.float32),
-            pltpu.SemaphoreType.DMA((2,)),
-            pltpu.SemaphoreType.DMA((early,)),
-        ],
-        compiler_params=params,
-        name="bring",
-    )(*kept(SMEM, item_pages, own_items), *kept(HBM, scales, cache_pages))
 
     partial_sums = pl.pallas_call(
         functools.partial(attend_kernel, slots, used, 1.0 / math.sqrt(head_size)),
-        out_shape=jax.ShapeDtypeStruct((beams * 2, slots, width), jnp.bfloat16),
-        in_specs=[spec(SMEM)] * 3 + [spec(VMEM)] * 2 + [spec(HBM)] * 2,
+        out_shape=VMEM((beams * 2, slots, width), jnp.bfloat16),
+        in_specs=[spec(SMEM)] * 3 + [spec(VMEM)] * 3 + [spec(HBM)],
         out_specs=spec(VMEM),
         scratch_shapes=[
-            VMEM((page_total - early,) + page_shape, jnp.bfloat16),
-            VMEM(out_weight.shape, jnp.bfloat16),
+            VMEM((16, 128), jnp.bfloat16),
             VMEM((len(used) * ITEM_ROWS, page_limit * page_rows), jnp.float32),
             VMEM((len(used) * ITEM_ROWS, page_limit * page_rows), jnp.bfloat16),
             VMEM((len(used) * ITEM_ROWS, head_size), jnp.float32),
             VMEM((items * ITEM_ROWS, head_size), jnp.float32),
-            pltpu.SemaphoreType.DMA((page_total - early,)),
-            pltpu.SemaphoreType.DMA((3,)),
+            pltpu.SemaphoreType.DMA((1,)),
         ],
         compiler_params=params,
         name="attend",
     )(
         *kept(SMEM, item_pages, item_lengths, scale_values),
-        *kept(VMEM, arrived.reshape(items, ITEM_ROWS, head_size), early_pages),
-        *kept(HBM, cache_pages, out_weight),
+        *kept(VMEM, arrived.reshape(items, ITEM_ROWS, head_size), pages, weight_head),
+        *kept(HBM, out_weight),
     )
 
     returned = lax.all_to_all(partial_sums, ("beam", "tp"), split_axis=0, concat_axis=0, tiled=True)

time: 33 us -> 32 us (0.970)
  blocking collectives: 9.73 us -> 23.7 us
  starting transfers between devices: 7.29 us -> 0 us
  waiting for transfers between devices: 4.39 us -> 0 us
  Pallas kernels: 11.3 us -> 8.06 us
    all_to_all x0 -> x1, blocking collectives: none -> 14 us  [on_device(): lax.all_to_all(send, 'beam', split_axis=0, concat_axis=0, tiled=True)]
    all_to_all x1 -> x0, starting transfers between devices: 7.29 us -> none  [on_device(): lax.all_to_all(send, 'beam', split_axis=0, concat_axis=0, tiled=True)]
    all_to_all x1 -> x0, waiting for transfers between devices: 4.39 us -> none  [on_device(): lax.all_to_all(send, 'beam', split_axis=0, concat_axis=0, tiled=True)]
    pallas_call x1, Pallas kernels: 5.85 us -> 2.32 us  [on_device(): pl.pallas_call(functools.partial(attend_kernel, slots, used, 1.0 / math.s...]
    pallas_call x1, Pallas kernels: 2.15 us -> 4.99 us  [on_device(): pl.pallas_call(functools.partial(pack_kernel, beams, slots, used), out_sh...]
    pallas_call x1 -> x0, Pallas kernels: 2.51 us -> none  [on_device(): pl.pallas_call(functools.partial(bring_kernel, slots), out_shape=(SMEM(sc...]
  transfers between devices with their start and end apart: 1 -> 0, of which waited for: 1 -> 0; matrix products, arithmetic and copies ran while one was open for 0% -> 0% of each run, Pallas kernels for 8% -> 0%
where the time goes in v3:
time: 32 us; the launch traced here: 31.8 us
  blocking collectives  23.7 us (74%)
  Pallas kernels  8.06 us (25%)
    all_to_all x1, blocking collectives, on_device(): lax.all_to_all(send, 'beam', split_axis=0, concat_axis=0, tiled=True)  14 us
    all_to_all x1, blocking collectives, on_device(): lax.all_to_all(partial_sums, ('beam', 'tp'), split_axis=0, concat_axis=0,...  9.73 us
    pallas_call x1, Pallas kernels, on_device(): pl.pallas_call(functools.partial(pack_kernel, beams, slots, used), out_sh...  4.99 us
    pallas_call x1, Pallas kernels, on_device(): pl.pallas_call(functools.partial(attend_kernel, slots, used, 1.0 / math.s...  2.32 us
    pallas_call x1, Pallas kernels, on_device(): pl.pallas_call(finish_kernel, out_shape=jax.ShapeDtypeStruct((children, w...  0.75 us

profile of v3, /device:TPU:0, one launch (start us, length us, event | category | flops | bytes accessed | tf_op | source)
XLA Modules:
  0.0 31.8 jit_solution(14906171042179331889)
XLA Ops:
  0.0 5.0 %pack.1 = (bf16[8,32,128]{2,1,0:T(8,128)(2,1)S(1)}, s32[48]{0:T(128)S(4)}, s32[16]{0:T(128)S(4)}, f32[4,48]{1,0:T(4,128)S(4)}, bf16[16,32]{1,0:T(8,128)(2,1)S(1)...) custom-call(s32[128]{0:T(128)} %parent_hbm.1, s32[128]{0:T(128)} %placement_hbm.1, ...), custom_call_target="tpu_custom_call" | custom-call | tf_op jit(solution)/shard_map/pack/pallas_call | solution.py:284
  5.0 14.0 %all_to_all.10 = bf16[8,32,128]{2,1,0:T(8,128)(2,1)S(1)} all-to-all(bf16[8,32,128]{2,1,0:T(8,128)(2,1)S(1)} %get-tuple-element.16), channel_id=1, replica_groups=mesh['grp'=2,'beam'=8,'tp'=2] {'beam'}, dimensions={0} | all-to-all | bytes 131072 | tf_op jit(solution)/shard_map/all_to_all | solution.py:327
  19.0 2.3 %attend.1 = bf16[16,2,1280]{2,1,0:T(2,128)(2,1)S(1)} custom-call(s32[48]{0:T(128)S(4)} %get-tuple-element.13.page_ref, s32[16]{0:T(128)S(4)} %get-tuple-element.14.item_length_ref, f32[4,48]{1,0:T(4,128)S(4)} %get-tuple-element.15.scale_ref, bf16[16,16,128]{2,1,0:T(8,128)(2,1)S(1)} %bitcast.7, bf16[48,2,2,128,128]{4,3,2,1,0:T(8,128)(2,1)S(1)} %get-tuple-element.17.pages_ref, ...), custom_call_target="tpu_custom_call" | custom-call | tf_op jit(solution)/shard_map/attend/pallas_call | solution.py:329
  21.3 9.7 %all_to_all.11.arrived_ref = bf16[16,2,1280]{2,1,0:T(2,128)(2,1)S(1)} all-to-all(bf16[16,2,1280]{2,1,0:T(2,128)(2,1)S(1)} %attend.1), channel_id=1, replica_groups=mesh['grp'=2,'beam'=8,'tp'=2] {'beam','tp'}, dimensions={0} | all-to-all | bytes 163840 | tf_op jit(solution)/shard_map/all_to_all | solution.py:350
  31.0 0.8 %finish.1 = bf16[16,1280]{1,0:T(8,128)(2,1)} custom-call(bf16[16,32]{1,0:T(8,128)(2,1)S(1)} %get-tuple-element.12.select_ref, bf16[16,2,1280]{2,1,0:T(2,128)(2,1)S(1)} %all_to_all.11.arrived_ref), custom_call_target="tpu_custom_call" | custom-call | tf_op jit(solution)/shard_map/finish/pallas_call | solution.py:352

commit v4 on v3

--- a/solution.py
+++ b/solution.py
@@ -50,8 +50,10 @@
     scale_in_ref,
     scale_wide_ref,
     item_ref,
+    asked_ref,
     count_ref,
     sem_ref,
+    page_sem_ref,
 ):
     heads, children, head_size = query_ref.shape
     entry_rows = entry_ref.shape[0]
@@ -66,8 +68,7 @@
             (table_hbm, table_ref),
             (length_hbm, length_ref),
             (scale_hbm, scale_in_ref),
-            (pages_hbm, pages_ref),
-            (weight_hbm.at[pl.ds(0, weight_ref.shape[0])], weight_ref),
+            (weight_hbm, weight_ref),
         ],
         sem_ref,
     )
@@ -85,8 +86,51 @@
     select_lane = lax.broadcasted_iota(jnp.int32, select_shape, 1)
     select_item = (select_lane // (2 * slots)) * slots + select_lane % slots
     wanted = jnp.zeros(select_shape, jnp.int32)
-    copies[0].wait()
-    copies[1].wait()
+    for copy in (copies[0], copies[1], copies[4], copies[5]):
+        copy.wait()
+
+    def one_index(index, _):
+        candidates = [placement_ref[parent_ref[index * children + child]] for child in range(children)]
+        place = index * slots
+        for slot in candidates:
+            item_ref[place] = slot % children
+            place = place + (slot // children == own).astype(jnp.int32)
+        return 0
+
+    for place in range(beams * slots):
+        item_ref[place] = 0
+    for local in range(children):
+        asked_ref[local] = 0
+    lax.fori_loop(0, beams, one_index, 0)
+    page_rows = pages_ref.shape[3]
+    for place, item in enumerate(used):
+        local = item_ref[item]
+        asked_ref[local] = 1
+        length = length_ref[own * children + local]
+        item_length_ref[place] = length
+        for page in range(page_limit):
+            kept_page = jnp.where(page * page_rows < length, page, 0)
+            page_ref[place * page_limit + page] = table_ref[kept_page, local]
+
+    def each_asked(act):
+        def one_slot(local, _):
+            length = length_ref[own * children + local]
+            for page in range(page_limit):
+
+                @pl.when((asked_ref[local] > 0) & (page * page_rows < length))
+                def _():
+                    number = table_ref[page, local]
+                    act(
+                        pltpu.make_async_copy(
+                            pages_hbm.at[number], pages_ref.at[number], page_sem_ref.at[local * page_limit + page]
+                        )
+                    )
+
+            return 0
+
+        lax.fori_loop(0, children, one_slot, 0)
+
+    each_asked(lambda copy: copy.start())
     own_slots = [placement_ref[parent_ref[own * children + child]] for child in range(children)]
     for child, slot in enumerate(own_slots):
         source = slot // children
@@ -112,28 +156,11 @@
     select_ref[...] = (select_item == wanted).astype(jnp.float32).astype(jnp.bfloat16)
     copies[6].wait()
     scale_wide_ref[...] = scale_in_ref[...].astype(jnp.float32)
-    scale_copy = pltpu.make_async_copy(scale_wide_ref, scale_ref, sem_ref.at[9])
+    scale_copy = pltpu.make_async_copy(scale_wide_ref, scale_ref, sem_ref.at[8])
     scale_copy.start()
-
-    def one_index(index, _):
-        asked = [placement_ref[parent_ref[index * children + child]] for child in range(children)]
-        place = index * slots
-        for slot in asked:
-            item_ref[place] = slot % children
-            place = place + (slot // children == own).astype(jnp.int32)
-        return 0
-
-    lax.fori_loop(0, beams, one_index, 0)
-    copies[4].wait()
-    copies[5].wait()
-    for place, item in enumerate(used):
-        local = item_ref[item]
-        item_length_ref[place] = length_ref[own * children + local]
-        for page in range(page_limit):
-            page_ref[place * page_limit + page] = table_ref[page, local]
     scale_copy.wait()
     copies[7].wait()
-    copies[8].wait()
+    each_asked(lambda copy: copy.wait())
 
 
 def attend_kernel(
@@ -146,20 +173,16 @@
     arrived_ref,
     pages_ref,
     weight_ref,
-    weight_hbm,
     out_ref,
-    weight_tail_ref,
     score_ref,
     rounded_ref,
     denominator_ref,
     attended_ref,
-    sem_ref,
 ):
     item_count = arrived_ref.shape[0]
     _, _, key_heads, page_rows, head_size = pages_ref.shape
     page_limit = page_ref.shape[0] // len(used)
-    cut, tail = weight_ref.shape[0], 0
-    heads = (cut + tail) // head_size
+    heads = weight_ref.shape[0] // head_size
     group = heads // key_heads
     row = lax.broadcasted_iota(jnp.int32, (ITEM_ROWS, head_size), 0)
     row_head = [(row >= head * group) & (row < (head + 1) * group) for head in range(key_heads)]
@@ -228,7 +251,7 @@
     attended = jnp.concatenate(
         [attended_ref[pl.ds(head, item_count, stride=ITEM_ROWS), :] for head in range(heads)], axis=1
     ).astype(jnp.bfloat16)
-    total = jnp.dot(attended[:, :cut], weight_ref[...], preferred_element_type=jnp.float32)
+    total = jnp.dot(attended, weight_ref[...], preferred_element_type=jnp.float32)
     total = total.astype(jnp.bfloat16)
     width = out_ref.shape[2]
     for half in range(2):
@@ -272,7 +295,6 @@
     items = beams * slots
     used = [index * slots + rank for index in range(beams) for rank in range(wanted)]
     page_total = len(used) * page_limit
-    cut = heads * head_size
     width = out_weight.shape[1] // 2
     limit = 16 * 1024 * 1024
     params = pltpu.CompilerParams(vmem_limit_bytes=limit)
@@ -281,7 +303,7 @@
     entry_rows = new_entries.reshape(children * 2 * key_heads, head_size)
     scales = jnp.transpose(cache_scales, (1, 2, 0)).reshape(2 * key_heads, page_count)
 
-    send, item_pages, item_lengths, scale_values, select, pages, weight_head = pl.pallas_call(
+    send, item_pages, item_lengths, scale_values, select, pages, weight = pl.pallas_call(
         functools.partial(pack_kernel, beams, slots, used),
         out_shape=(
             VMEM((beams, slots * ITEM_ROWS, head_size), jnp.bfloat16),
@@ -290,7 +312,7 @@
             SMEM(scales.shape, jnp.float32),
             VMEM((children, 2 * items), jnp.bfloat16),
             VMEM(cache_pages.shape, jnp.bfloat16),
-            VMEM((cut, out_weight.shape[1]), jnp.bfloat16),
+            VMEM(out_weight.shape, jnp.bfloat16),
         ),
         in_specs=[spec(HBM)] * 9,
         out_specs=(spec(VMEM),) + (spec(SMEM),) * 3 + (spec(VMEM),) * 3,
@@ -304,8 +326,10 @@
             VMEM(scales.shape, jnp.bfloat16),
             VMEM(scales.shape, jnp.float32),
             SMEM((items + 1,), jnp.int32),
+            SMEM((children,), jnp.int32),
             SMEM((beams,), jnp.int32),
-            pltpu.SemaphoreType.DMA((10,)),
+            pltpu.SemaphoreType.DMA((9,)),
+            pltpu.SemaphoreType.DMA((children * page_limit,)),
         ],
         compiler_params=params,
         name="pack",
@@ -329,22 +353,19 @@
     partial_sums = pl.pallas_call(
         functools.partial(attend_kernel, slots, used, 1.0 / math.sqrt(head_size)),
         out_shape=VMEM((beams * 2, slots, width), jnp.bfloat16),
-        in_specs=[spec(SMEM)] * 3 + [spec(VMEM)] * 3 + [spec(HBM)],
+        in_specs=[spec(SMEM)] * 3 + [spec(VMEM)] * 3,
         out_specs=spec(VMEM),
         scratch_shapes=[
-            VMEM((16, 128), jnp.bfloat16),
             VMEM((len(used) * ITEM_ROWS, page_limit * page_rows), jnp.float32),
             VMEM((len(used) * ITEM_ROWS, page_limit * page_rows), jnp.bfloat16),
             VMEM((len(used) * ITEM_ROWS, head_size), jnp.float32),
             VMEM((items * ITEM_ROWS, head_size), jnp.float32),
-            pltpu.SemaphoreType.DMA((1,)),
         ],
         compiler_params=params,
         name="attend",
     )(
         *kept(SMEM, item_pages, item_lengths, scale_values),
-        *kept(VMEM, arrived.reshape(items, ITEM_ROWS, head_size), pages, weight_head),
-        *kept(HBM, out_weight),
+        *kept(VMEM, arrived.reshape(items, ITEM_ROWS, head_size), pages, weight),
     )
 
     returned = lax.all_to_all(partial_sums, ("beam", "tp"), split_axis=0, concat_axis=0, tiled=True)

time: 32 us -> 31.5 us (0.984)
  Pallas kernels: 8.06 us -> 7.72 us
    pallas_call x1, Pallas kernels: 4.99 us -> 4.66 us  [on_device(): pl.pallas_call(functools.partial(pack_kernel, beams, slots, used), out_sh...]
where the time goes in v4:
time: 31.5 us
  blocking collectives  23.8 us (76%)
  Pallas kernels  7.72 us (25%)
    all_to_all x1, blocking collectives, on_device(): lax.all_to_all(send, 'beam', split_axis=0, concat_axis=0, tiled=True)  14.1 us
    all_to_all x1, blocking collectives, on_device(): lax.all_to_all(partial_sums, ('beam', 'tp'), split_axis=0, concat_axis=0,...  9.73 us
    pallas_call x1, Pallas kernels, on_device(): pl.pallas_call(functools.partial(pack_kernel, beams, slots, used), out_sh...  4.66 us
    pallas_call x1, Pallas kernels, on_device(): pl.pallas_call(functools.partial(attend_kernel, slots, used, 1.0 / math.s...  2.31 us
    pallas_call x1, Pallas kernels, on_device(): pl.pallas_call(finish_kernel, out_shape=jax.ShapeDtypeStruct((children, w...  0.75 us

profile of v4, /device:TPU:0, one launch (start us, length us, event | category | flops | bytes accessed | tf_op | source)
XLA Modules:
  0.0 31.5 jit_solution(1829594471571270539)
XLA Ops:
  0.0 4.7 %pack.1 = (bf16[8,32,128]{2,1,0:T(8,128)(2,1)S(1)}, s32[48]{0:T(128)S(4)}, s32[16]{0:T(128)S(4)}, f32[4,48]{1,0:T(4,128)S(4)}, bf16[16,32]{1,0:T(8,128)(2,1)S(1)...) custom-call(s32[128]{0:T(128)} %parent_hbm.1, s32[128]{0:T(128)} %placement_hbm.1, ...), custom_call_target="tpu_custom_call" | custom-call | tf_op jit(solution)/shard_map/pack/pallas_call | solution.py:306
  4.7 14.1 %all_to_all.10 = bf16[8,32,128]{2,1,0:T(8,128)(2,1)S(1)} all-to-all(bf16[8,32,128]{2,1,0:T(8,128)(2,1)S(1)} %get-tuple-element.16), channel_id=1, replica_groups=mesh['grp'=2,'beam'=8,'tp'=2] {'beam'}, dimensions={0} | all-to-all | bytes 131072 | tf_op jit(solution)/shard_map/all_to_all | solution.py:351
  18.7 2.3 %attend.1 = bf16[16,2,1280]{2,1,0:T(2,128)(2,1)S(1)} custom-call(s32[48]{0:T(128)S(4)} %get-tuple-element.13.page_ref, s32[16]{0:T(128)S(4)} %get-tuple-element.14.item_length_ref, f32[4,48]{1,0:T(4,128)S(4)} %get-tuple-element.15.scale_ref, bf16[16,16,128]{2,1,0:T(8,128)(2,1)S(1)} %bitcast.7, bf16[48,2,2,128,128]{4,3,2,1,0:T(8,128)(2,1)S(1)} %get-tuple-element.17.pages_ref, ...), custom_call_target="tpu_custom_call" | custom-call | tf_op jit(solution)/shard_map/attend/pallas_call | solution.py:353
  21.0 9.7 %all_to_all.11.arrived_ref = bf16[16,2,1280]{2,1,0:T(2,128)(2,1)S(1)} all-to-all(bf16[16,2,1280]{2,1,0:T(2,128)(2,1)S(1)} %attend.1), channel_id=1, replica_groups=mesh['grp'=2,'beam'=8,'tp'=2] {'beam','tp'}, dimensions={0} | all-to-all | bytes 163840 | tf_op jit(solution)/shard_map/all_to_all | solution.py:371
  30.8 0.8 %finish.1 = bf16[16,1280]{1,0:T(8,128)(2,1)} custom-call(bf16[16,32]{1,0:T(8,128)(2,1)S(1)} %get-tuple-element.12.select_ref, bf16[16,2,1280]{2,1,0:T(2,128)(2,1)S(1)} %all_to_all.11.arrived_ref), custom_call_target="tpu_custom_call" | custom-call | tf_op jit(solution)/shard_map/finish/pallas_call | solution.py:373

commit v5 on v3

--- a/solution.py
+++ b/solution.py
@@ -33,14 +33,12 @@
     length_hbm,
     scale_hbm,
     pages_hbm,
-    weight_hbm,
     send_ref,
     page_ref,
     item_length_ref,
     scale_ref,
     select_ref,
     pages_ref,
-    weight_ref,
     parent_ref,
     placement_ref,
     query_ref,
@@ -67,7 +65,6 @@
             (length_hbm, length_ref),
             (scale_hbm, scale_in_ref),
             (pages_hbm, pages_ref),
-            (weight_hbm.at[pl.ds(0, weight_ref.shape[0])], weight_ref),
         ],
         sem_ref,
     )
@@ -81,7 +78,8 @@
     query_row = query_lane // children
     entry_row = entry_lane % per_child + heads
     select_shape = select_ref.shape
-    child_row = lax.broadcasted_iota(jnp.int32, select_shape, 0)
+    select_row = lax.broadcasted_iota(jnp.int32, select_shape, 0)
+    child_row = select_row % children
     select_lane = lax.broadcasted_iota(jnp.int32, select_shape, 1)
     select_item = (select_lane // (2 * slots)) * slots + select_lane % slots
     wanted = jnp.zeros(select_shape, jnp.int32)
@@ -109,10 +107,11 @@
     )
     moved += jnp.dot(entry_pick, entry_ref[...], preferred_element_type=jnp.float32)
     send_ref[...] = moved.astype(jnp.bfloat16).reshape(send_ref.shape)
-    select_ref[...] = (select_item == wanted).astype(jnp.float32).astype(jnp.bfloat16)
+    picked = (select_item == wanted) & ((select_lane // slots) % 2 == select_row // children)
+    select_ref[...] = picked.astype(jnp.float32).astype(jnp.bfloat16)
     copies[6].wait()
     scale_wide_ref[...] = scale_in_ref[...].astype(jnp.float32)
-    scale_copy = pltpu.make_async_copy(scale_wide_ref, scale_ref, sem_ref.at[9])
+    scale_copy = pltpu.make_async_copy(scale_wide_ref, scale_ref, sem_ref.at[8])
     scale_copy.start()
 
     def one_index(index, _):
@@ -133,7 +132,6 @@
             page_ref[place * page_limit + page] = table_ref[page, local]
     scale_copy.wait()
     copies[7].wait()
-    copies[8].wait()
 
 
 def attend_kernel(
@@ -145,21 +143,16 @@
     scale_ref,
     arrived_ref,
     pages_ref,
-    weight_ref,
-    weight_hbm,
     out_ref,
-    weight_tail_ref,
     score_ref,
     rounded_ref,
     denominator_ref,
     attended_ref,
-    sem_ref,
 ):
     item_count = arrived_ref.shape[0]
     _, _, key_heads, page_rows, head_size = pages_ref.shape
     page_limit = page_ref.shape[0] // len(used)
-    cut, tail = weight_ref.shape[0], 0
-    heads = (cut + tail) // head_size
+    heads = out_ref.shape[2] // head_size
     group = heads // key_heads
     row = lax.broadcasted_iota(jnp.int32, (ITEM_ROWS, head_size), 0)
     row_head = [(row >= head * group) & (row < (head + 1) * group) for head in range(key_heads)]
@@ -228,18 +221,24 @@
     attended = jnp.concatenate(
         [attended_ref[pl.ds(head, item_count, stride=ITEM_ROWS), :] for head in range(heads)], axis=1
     ).astype(jnp.bfloat16)
-    total = jnp.dot(attended[:, :cut], weight_ref[...], preferred_element_type=jnp.float32)
-    total = total.astype(jnp.bfloat16)
-    width = out_ref.shape[2]
     for half in range(2):
         for index in range(item_count // slots):
-            out_ref[index * 2 + half] = total[index * slots : (index + 1) * slots, half * width : (half + 1) * width]
-
-
-def finish_kernel(select_ref, arrived_ref, out_ref):
-    members, slots, width = arrived_ref.shape
-    parts = arrived_ref[...].reshape(members * slots, width)
-    out_ref[...] = jnp.dot(select_ref[...], parts, preferred_element_type=jnp.float32).astype(out_ref.dtype)
+            out_ref[index * 2 + half] = attended[index * slots : (index + 1) * slots]
+
+
+def finish_kernel(select_ref, arrived_ref, own_weight_ref, other_weight_ref, out_ref):
+    members, slots, depth = arrived_ref.shape
+    children, width = out_ref.shape
+    parts = arrived_ref[...].reshape(members * slots, depth)
+    ordered = jnp.dot(select_ref[...], parts, preferred_element_type=jnp.float32).astype(jnp.bfloat16)
+    half = lax.axis_index("tp")
+    low, high = ordered[:children], ordered[children:]
+    own = jnp.where(half == 0, low, high)
+    other = jnp.where(half == 0, high, low)
+    columns = pl.ds(pl.multiple_of(half * width, 128), width)
+    total = jnp.dot(own, own_weight_ref[:, columns], preferred_element_type=jnp.float32)
+    total += jnp.dot(other, other_weight_ref[:, columns], preferred_element_type=jnp.float32)
+    out_ref[...] = total.astype(out_ref.dtype)
 
 
 def kept(space, *arrays):
@@ -272,7 +271,6 @@
     items = beams * slots
     used = [index * slots + rank for index in range(beams) for rank in range(wanted)]
     page_total = len(used) * page_limit
-    cut = heads * head_size
     width = out_weight.shape[1] // 2
     limit = 16 * 1024 * 1024
     params = pltpu.CompilerParams(vmem_limit_bytes=limit)
@@ -281,19 +279,20 @@
     entry_rows = new_entries.reshape(children * 2 * key_heads, head_size)
     scales = jnp.transpose(cache_scales, (1, 2, 0)).reshape(2 * key_heads, page_count)
 
-    send, item_pages, item_lengths, scale_values, select, pages, weight_head = pl.pallas_call(
+    swap = [(half, 1 - half) for half in range(2)]
+    other_weight = lax.ppermute(out_weight, "tp", swap)
+    send, item_pages, item_lengths, scale_values, select, pages = pl.pallas_call(
         functools.partial(pack_kernel, beams, slots, used),
         out_shape=(
             VMEM((beams, slots * ITEM_ROWS, head_size), jnp.bfloat16),
             SMEM((page_total,), jnp.int32),
             SMEM((len(used),), jnp.int32),
             SMEM(scales.shape, jnp.float32),
-            VMEM((children, 2 * items), jnp.bfloat16),
+            VMEM((2 * children, 2 * items), jnp.bfloat16),
             VMEM(cache_pages.shape, jnp.bfloat16),
-            VMEM((cut, out_weight.shape[1]), jnp.bfloat16),
         ),
-        in_specs=[spec(HBM)] * 9,
-        out_specs=(spec(VMEM),) + (spec(SMEM),) * 3 + (spec(VMEM),) * 3,
+        in_specs=[spec(HBM)] * 8,
+        out_specs=(spec(VMEM),) + (spec(SMEM),) * 3 + (spec(VMEM),) * 2,
         scratch_shapes=[
             SMEM(parent.shape, jnp.int32),
             SMEM(placement.shape, jnp.int32),
@@ -305,7 +304,7 @@
             VMEM(scales.shape, jnp.float32),
             SMEM((items + 1,), jnp.int32),
             SMEM((beams,), jnp.int32),
-            pltpu.SemaphoreType.DMA((10,)),
+            pltpu.SemaphoreType.DMA((9,)),
         ],
         compiler_params=params,
         name="pack",
@@ -320,43 +319,41 @@
             lengths,
             scales,
             cache_pages,
-            out_weight,
         )
     )
 
     arrived = lax.all_to_all(send, "beam", split_axis=0, concat_axis=0, tiled=True)
 
-    partial_sums = pl.pallas_call(
+    arrived, sent_back = lax.optimization_barrier((arrived, other_weight))
+    own_weight = lax.ppermute(sent_back, "tp", swap)
+    attended = pl.pallas_call(
         functools.partial(attend_kernel, slots, used, 1.0 / math.sqrt(head_size)),
-        out_shape=VMEM((beams * 2, slots, width), jnp.bfloat16),
-        in_specs=[spec(SMEM)] * 3 + [spec(VMEM)] * 3 + [spec(HBM)],
+        out_shape=VMEM((beams * 2, slots, heads * head_size), jnp.bfloat16),
+        in_specs=[spec(SMEM)] * 3 + [spec(VMEM)] * 2,
         out_specs=spec(VMEM),
         scratch_shapes=[
-            VMEM((16, 128), jnp.bfloat16),
             VMEM((len(used) * ITEM_ROWS, page_limit * page_rows), jnp.float32),
             VMEM((len(used) * ITEM_ROWS, page_limit * page_rows), jnp.bfloat16),
             VMEM((len(used) * ITEM_ROWS, head_size), jnp.float32),
             VMEM((items * ITEM_ROWS, head_size), jnp.float32),
-            pltpu.SemaphoreType.DMA((1,)),
         ],
         compiler_params=params,
         name="attend",
     )(
         *kept(SMEM, item_pages, item_lengths, scale_values),
-        *kept(VMEM, arrived.reshape(items, ITEM_ROWS, head_size), pages, weight_head),
-        *kept(HBM, out_weight),
-    )
-
-    returned = lax.all_to_all(partial_sums, ("beam", "tp"), split_axis=0, concat_axis=0, tiled=True)
+        *kept(VMEM, arrived.reshape(items, ITEM_ROWS, head_size), pages),
+    )
+
+    returned = lax.all_to_all(attended, ("beam", "tp"), split_axis=0, concat_axis=0, tiled=True)
 
     return pl.pallas_call(
         finish_kernel,
         out_shape=jax.ShapeDtypeStruct((children, width), jnp.bfloat16),
-        in_specs=[spec(VMEM)] * 2,
+        in_specs=[spec(VMEM)] * 4,
         out_specs=spec(VMEM),
         compiler_params=params,
         name="finish",
-    )(*kept(VMEM, select, returned))
+    )(*kept(VMEM, select, returned, own_weight, other_weight))
 
 
 def solution(mesh):

time: 32 us -> 30 us (0.938)
  Pallas kernels: 8.06 us -> 6 us
  starting transfers between devices: 0 us -> 0.46 us
  blocking collectives: 23.7 us -> 23.3 us
    pallas_call x1, Pallas kernels: 4.99 us -> 2.92 us  [on_device(): pl.pallas_call(functools.partial(pack_kernel, beams, slots, used), out_sh...]
    pallas_call x1, Pallas kernels: 0.75 us -> 1.69 us  [on_device(): pl.pallas_call(finish_kernel, out_shape=jax.ShapeDtypeStruct((children, w...]
    pallas_call x1, Pallas kernels: 2.32 us -> 1.39 us  [on_device(): pl.pallas_call(functools.partial(attend_kernel, slots, used, 1.0 / math.s...]
    ppermute x0 -> x2, starting transfers between devices: none -> 0.46 us  [the longest x1 0.45 us: on_device(): other_weight = lax.ppermute(out_weight, 'tp', swap)]
    all_to_all x1, blocking collectives: 14 us -> 13.5 us  [on_device(): lax.all_to_all(send, 'beam', split_axis=0, concat_axis=0, tiled=True)]
  transfers between devices with their start and end apart: 0 -> 2, of which waited for: 0 -> 0; matrix products, arithmetic and copies ran while one was open for 0% -> 0% of each run, Pallas kernels for 0% -> 15%
where the time goes in v5:
time: 30 us; the launch traced here: 29.7 us
  blocking collectives  23.3 us (78%)
  Pallas kernels  6 us (20%)
  starting transfers between devices  0.46 us (2%)
    all_to_all x1, blocking collectives, on_device(): lax.all_to_all(send, 'beam', split_axis=0, concat_axis=0, tiled=True)  13.5 us
    all_to_all x1, blocking collectives, on_device(): lax.all_to_all(attended, ('beam', 'tp'), split_axis=0, concat_axis=0, til...  9.73 us
    pallas_call x1, Pallas kernels, on_device(): pl.pallas_call(functools.partial(pack_kernel, beams, slots, used), out_sh...  2.92 us
    pallas_call x1, Pallas kernels, on_device(): pl.pallas_call(finish_kernel, out_shape=jax.ShapeDtypeStruct((children, w...  1.69 us
    pallas_call x1, Pallas kernels, on_device(): pl.pallas_call(functools.partial(attend_kernel, slots, used, 1.0 / math.s...  1.39 us
  transfers between devices with their start and end apart: 2, of which 0 were waited for; matrix products, arithmetic and copies ran while one was open for 0% of the time, Pallas kernels for 15%

profile of v5, /device:TPU:0, one launch (start us, length us, event | category | flops | bytes accessed | tf_op | source)
XLA Modules:
  0.0 29.7 jit_solution(3811038275923947774)
XLA Ops:
  0.0 0.5 %collective-permute-start = (bf16[1280,2560]{1,0:T(8,128)(2,1)}, bf16[1280,2560]{1,0:T(8,128)(2,1)S(1)}, u32[]{:S(2)}, u32[]{:S(2)}) collective-permute-start(bf16[1280,2560]{1,0:T(8,128)(2,1)} %param.17), channel_id=1, source_target_pairs={{0,1},{1,0},{2,3},{3,2},{4,5},{5,4},{6,7},{7,6},{8,9},{9,8},{10,11... | collective-permute-start | bytes 19660808 | tf_op jit(solution)/shard_map/ppermute | solution.py:283
  0.5 2.9 %pack.1 = (bf16[8,32,128]{2,1,0:T(8,128)(2,1)S(1)}, s32[48]{0:T(128)S(4)}, s32[16]{0:T(128)S(4)}, f32[4,48]{1,0:T(4,128)S(4)}, bf16[32,32]{1,0:T(8,128)(2,1)S(1)}, /*index=5*/bf16[48,2,2,128,128]{4,3,2,1,0:T(8,128)(2,1)S(1)}) custom-call(s32[128]{0:T(128)} %parent_hbm.1, s32[128]{0:T(128)} %placement_hbm.1, bf16[10,16,128]{2,1,0:T(8,128)(2,1)} %bitcast.8, ...), custom_call_target="tpu_custom_call" | custom-call | tf_op jit(solution)/shard_map/pack/pallas_call | solution.py:284
  3.4 13.5 %all_to_all.10 = bf16[8,32,128]{2,1,0:T(8,128)(2,1)S(1)} all-to-all(bf16[8,32,128]{2,1,0:T(8,128)(2,1)S(1)} %get-tuple-element.17), channel_id=1, replica_groups=mesh['grp'=2,'beam'=8,'tp'=2] {'beam'}, dimensions={0} | all-to-all | bytes 131072 | tf_op jit(solution)/shard_map/all_to_all | solution.py:325
  16.9 0.0 collective-permute-done.other_weight_ref
  16.9 0.0 collective-permute-start.1
  16.9 1.4 %attend.1 = bf16[16,2,1280]{2,1,0:T(2,128)(2,1)S(1)} custom-call(s32[48]{0:T(128)S(4)} %get-tuple-element.14.page_ref, s32[16]{0:T(128)S(4)} %get-tuple-element.15.item_length_ref, f32[4,48]{1,0:T(4,128)S(4)} %get-tuple-element.16.scale_ref, bf16[16,16,128]{2,1,0:T(8,128)(2,1)S(1)} %bitcast.7, bf16[48,2,2,128,128]{4,3,2,1,0:T(8,128)(2,1)S(1)} %get-tuple-element.19.pages_ref), custom_call_target="tpu_custom_call" | custom-call | tf_op jit(solution)/shard_map/attend/pallas_call | solution.py:329
  18.3 9.7 %all_to_all.11.arrived_ref = bf16[16,2,1280]{2,1,0:T(2,128)(2,1)S(1)} all-to-all(bf16[16,2,1280]{2,1,0:T(2,128)(2,1)S(1)} %attend.1), channel_id=1, replica_groups=mesh['grp'=2,'beam'=8,'tp'=2] {'beam','tp'}, dimensions={0} | all-to-all | bytes 163840 | tf_op jit(solution)/shard_map/all_to_all | solution.py:347
  28.1 0.0 collective-permute-done.1.own_weight_ref
  28.1 1.7 %finish.1 = bf16[16,1280]{1,0:T(8,128)(2,1)} custom-call(bf16[32,32]{1,0:T(8,128)(2,1)S(1)} %get-tuple-element.13.select_ref, bf16[16,2,1280]{2,1,0:T(2,128)(2,1)S(1)} %all_to_all.11.arrived_ref, bf16[1280,2560]{1,0:T(8,128)(2,1)S(1)} %collective-permute-done.1.own_weight_ref, bf16[1280,2560]{1,0:T(8,128)(2,1)S(1)} %collective-permute-done.other_weight_ref), custom_call_target="tpu_custom_call" | custom-call | tf_op jit(solution)/shard_map/finish/pallas_call | solution.py:349
Async XLA Ops:
  0.0 16.9 %collective-permute-start = (bf16[1280,2560]{1,0:T(8,128)(2,1)}, bf16[1280,2560]{1,0:T(8,128)(2,1)S(1)}, u32[]{:S(2)}, u32[]{:S(2)}) collective-permute-start(bf16[1280,2560]{1,0:T(8,128)(2,1)} %param.17), channel_id=1, source_target_pairs={{0,1},{1,0},{2,3},{3,2},{4,5},{5,4},{6,7},{7,6},{8,9},{9,8},{10,11... | collective-permute-start | bytes 19660808 | tf_op jit(solution)/shard_map/ppermute | solution.py:283
  16.9 11.1 %collective-permute-start.1 = (bf16[1280,2560]{1,0:T(8,128)(2,1)S(1)}, bf16[1280,2560]{1,0:T(8,128)(2,1)S(1)}, u32[]{:S(2)}, u32[]{:S(2)}) collective-permute-start(bf16[1280,2560]{1,0:T(8,128)(2,1)S(1)} %collective-permute-done.other_weight_ref), channel_id=1, source_target_pairs={{0,1},{1,0},{2,3},{3,2},{4,5},{5,4},{6,7},{7,6},{8,9},{9,8},{10,11... | collective-permute-start | bytes 19660808 | tf_op jit(solution)/shard_map/ppermute | solution.py:328
